TPU v7x, 32 devices: a whole 2x2x4 slice. The times are simulated.
32 devices in a mesh: ab: 16 (over z, y, x), cd: 2 (over core).
Axes of the slice: x: 2, y: 2, z: 4, core: 2. Of those that a mesh axis runs over, the one named last changes fastest.
Arguments:
- amplitudes: bfloat16 [48, 16, 3072], P('ab', None, 'cd'), may hold values from -6 to 6
- integral: bfloat16 [49152, 20480], P('ab', 'cd'), may hold values from -0.02734375 to 0.02734375
Outputs:
- ladder: float32 [48, 20480], P('ab', 'cd')
All inputs are finite; a program needn't handle non-finite values.
Results may differ from a plain program's by a relative error of at most 0.0003.
Values may be sent and summed in bfloat16 or wider, within the bound.
No kernel may reach another device: no remote copies, remote signals or barrier semaphores. Data moves between devices by JAX's collectives and lax.ppermute only.
A program may use at most 128 MiB of HBM per device.

v0:
```python
import jax
import jax.numpy as jnp
from jax import lax
from jax.sharding import PartitionSpec as P


def per_device(amplitudes, integral):
    widened = lax.all_gather(amplitudes, "cd", axis=2, tiled=True)
    window = lax.all_to_all(widened, "ab", split_axis=1, concat_axis=0, tiled=True)
    window = window.reshape(window.shape[0], window.shape[2])
    return lax.psum_scatter(
        jnp.dot(window, integral, preferred_element_type=jnp.float32),
        "ab",
        scatter_dimension=0,
        tiled=True,
    )


def solution(mesh):
    placed = (P("ab", None, "cd"), P("ab", "cd"))
    return jax.shard_map(
        per_device, mesh=mesh, in_specs=placed, out_specs=P("ab", "cd"), check_vma=False
    )
```

profile of v0, /device:TPU:0, one launch (start us, length us, event | category | flops | bytes accessed | tf_op | source)
XLA Modules:
  0.0 185.6 jit_solution(9200657306830088556)
XLA Ops:
  6.5 0.0 copy-start
  6.5 0.0 all-reduce.3.cloned.1.call-start
  6.5 1.0 copy.4
  7.6 2.2 %all_gather.3 = bf16[3,16,3072]{2,0,1:T(4,128)(2,1)S(1)} all-gather(bf16[3,16,1536]{2,0,1:T(4,128)(2,1)S(1)} %copy.4), channel_id=1, replica_groups=mesh['ab'=16,'cd'=2] {'cd'}, dimensions={2}, use_global_device_ids=true | all-gather | bytes 442368 | tf_op jit(solution)/shard_map/all_gather | solution.py:8
  9.8 20.9 %all_to_all.15 = bf16[3,16,3072]{2,0,1:T(4,128)(2,1)S(1)} all-to-all(bf16[3,16,3072]{2,0,1:T(4,128)(2,1)S(1)} %all_gather.3), channel_id=1, replica_groups=mesh['ab'=16,'cd'=2] {'ab'}, dimensions={1} | all-to-all | bytes 589824 | tf_op jit(solution)/shard_map/all_to_all | solution.py:9
  30.7 0.2 reshape.4
  30.9 24.2 %fusion = f32[48,10240]{1,0:T(8,128)} fusion(bf16[48,3072]{1,0:T(8,128)(2,1)S(1)} %reshape.4, bf16[3072,10240]{1,0:T(8,128)(2,1)} %param.3), kind=kOutput, calls=%fused_computation.1 | convolution fusion | flops 3019898880 | bytes 65175552 | tf_op jit(solution)/shard_map/dot_general | solution.py:12
  55.1 0.0 all-reduce.3.cloned.1.call-update
  55.1 0.0 copy-done
  55.1 0.6 dynamic-slice
  56.4 120.5 %all-reduce.3.cloned.1.call-done = f32[48,10240]{1,0:T(8,128)} async-done(((f32[48,10240]{1,0:T(8,128)}), f32[48,10240]{1,0:T(8,128)}) %all-reduce.3.cloned.1.call-update) | async-done | bytes 1966096
  176.9 1.8 constant_dynamic-slice_fusion
Async XLA Ops:
  6.5 48.6 %copy-start = (u32[32]{0:T(128)S(1)}, u32[32]{0:T(128)}, u32[]{:S(2)}) copy-start(u32[32]{0:T(128)} %constant.3) | copy-start | bytes 388
  6.5 170.4 %all-reduce.3.cloned.1.call-start = ((), (), s32[]{:S(2)}) async-start(), calls=%async_computation.1 | async-start | bytes 3932160
Sparse Core Ops, SparseCore 0:
  55.2 121.6 all-reduce.2
where the time goes:
time: 186 us
  waiting for transfers between devices  121 us (65%)
  matrix products  24.2 us (13%)
  blocking collectives  23.1 us (12%)
  between operations  14.1 us (8%)
  local copies, waits for them, and re-layouts  3.67 us (2%)
    unnamed x2, waiting for transfers between devices  121 us
    dot_general x1, matrix products, per_device(): jnp.dot(window, integral, preferred_element_type=jnp.float32)  24.2 us
    all_to_all x1, blocking collectives, per_device(): lax.all_to_all(widened, 'ab', split_axis=1, concat_axis=0, tiled=True)  20.9 us
  transfers between devices with their start and end apart: 1, of which 1 were waited for; matrix products, arithmetic and copies ran while one was open for 0% of the time, Pallas kernels for 0%

commit v1 on v0

v1 whole, which is shorter than its diff:
```python
import functools
import math

import jax
import jax.numpy as jnp
from jax import lax
from jax.experimental import pallas as pl
from jax.experimental.pallas import tpu as pltpu
from jax.sharding import PartitionSpec as P

F32, BF16 = jnp.float32, jnp.bfloat16
PLANE = 4
UNITS = 20
AHEAD = (2, 5)
STREAM = 7
SECOND = 6
MORE = 2
SLOTS = 4
PIECES = 4
TILE = 512
MATRIX = 256
LANES = 128
TOP, TINY = 1440.0, 1e-30
SMALL = pl.CostEstimate(flops=1 << 20, bytes_accessed=1 << 20, transcendentals=0)
VMEM = 14 << 20


def select(rows, columns, source):
    row = lax.broadcasted_iota(jnp.int32, (rows, columns), 0)
    column = lax.broadcasted_iota(jnp.int32, (rows, columns), 1)
    return (column == source(row)).astype(BF16)


def copies(integral, start, unit, target, sems):
    step = target.shape[0] // PIECES
    return [
        pltpu.make_async_copy(
            integral.at[pl.ds(i * step, step), pl.ds(start, unit)],
            target.at[pl.ds(i * step, step), :],
            sems.at[i],
        )
        for i in range(PIECES)
    ]


def load(start, columns, unit, integral, after):
    depth = integral.shape[0]

    def kernel(integral_ref, after_ref, out_ref, sems):
        moves = []
        for k in range(columns // unit):
            target = out_ref.at[:, pl.ds(k * unit, unit)]
            moves += copies(integral_ref, start + k * unit, unit, target, sems.at[k])
        for move in moves:
            move.start()
        for move in moves:
            move.wait()

    return pl.pallas_call(
        kernel,
        out_shape=pltpu.VMEM((depth, columns), BF16),
        in_specs=[pl.BlockSpec(memory_space=pl.ANY)] * 2,
        out_specs=pl.BlockSpec(memory_space=pltpu.VMEM),
        scratch_shapes=[pltpu.SemaphoreType.DMA((columns // unit, PIECES))],
        compiler_params=pltpu.CompilerParams(vmem_limit_bytes=VMEM),
        cost_estimate=pl.CostEstimate(flops=0, bytes_accessed=depth * columns * 2, transcendentals=0),
    )(integral, after)


def encode(sums, largest):
    scale = (TOP / jnp.maximum(largest, TINY)).astype(BF16)
    scaled = sums * scale.astype(F32)
    square = scaled * scaled
    fourth = square * square
    return (fourth * fourth * square * (scaled * jnp.abs(scaled))).astype(BF16), scale


def decode(code, scale):
    code = code.astype(F32)
    size = jnp.exp2(jnp.log2(jnp.abs(code)) * (1.0 / 12.0)) * (1.0 / scale.astype(F32))
    return jnp.where(code < 0, -size, size)


def fold(group):
    return 8 // math.gcd(group, 8)


def packed_rows(group, part):
    whole = group // 8 * 8
    rest = group - whole
    rows = [(0, whole, part * whole)] if whole else []
    return rows + ([(whole, rest, fold(group) * whole + part * rest)] if rest else [])


def unpacked(array, group, start, count):
    parts = fold(group)
    whole = group // 8 * 8
    rest = group - whole
    out = []
    for j in range(parts):
        pieces = []
        if start < whole:
            pieces.append(array[j * whole + start : j * whole + min(start + count, whole)])
        if start + count > whole:
            at = parts * whole + j * rest - whole
            pieces.append(array[at + max(start, whole) : at + start + count])
        out.append(pieces[0] if len(pieces) == 1 else jnp.concatenate(pieces, axis=0))
    return out


def split_by_plane(halves, lines):
    pairs, blocks, offsets = halves[0].shape
    cores, group = len(halves), lines * pairs
    rows = cores * group

    def kernel(*refs):
        me, core = lax.axis_index("ab"), lax.axis_index("cd")
        total = 0.0
        for j, ref in enumerate(refs[:cores]):

            def source(row):
                r, h, s, p = row // rows, row % rows // group, row % group // pairs, row % pairs
                column = p * blocks + jnp.bitwise_xor(s * PLANE + r, me)
                return jnp.where(h == jnp.bitwise_xor(core, j), column, -1)

            flat = ref[...].reshape(pairs * blocks, offsets)
            total += jnp.dot(select(PLANE * rows, pairs * blocks, source), flat, preferred_element_type=F32)
        for r, out in enumerate(refs[cores:]):
            out[...] = total[r * rows : (r + 1) * rows].astype(BF16)

    shape = jax.ShapeDtypeStruct((rows, offsets), BF16)
    return pl.pallas_call(
        kernel,
        out_shape=[shape] * PLANE,
        in_specs=[pl.BlockSpec(memory_space=pltpu.VMEM)] * cores,
        out_specs=[pl.BlockSpec(memory_space=pltpu.VMEM)] * PLANE,
        compiler_params=pltpu.CompilerParams(vmem_limit_bytes=VMEM),
        cost_estimate=SMALL,
    )(*halves)


def split_by_line(parts, cores, lines, pairs, after):
    offsets = parts[0].shape[1]
    group, rows = lines * pairs, cores * PLANE * pairs

    def kernel(*refs):
        total = 0.0
        for r, ref in enumerate(refs[:PLANE]):

            def source(row):
                s, h, at, p = row // rows, row % rows // (PLANE * pairs), row % rows // pairs % PLANE, row % pairs
                return jnp.where(at == r, h * group + s * pairs + p, -1)

            total += jnp.dot(select(lines * rows, cores * group, source), ref[...], preferred_element_type=F32)
        for s, out in enumerate(refs[PLANE + 1 :]):
            out[...] = total[s * rows : (s + 1) * rows].astype(BF16)

    shape = jax.ShapeDtypeStruct((rows, offsets), BF16)
    return pl.pallas_call(
        kernel,
        out_shape=[shape] * lines,
        in_specs=[pl.BlockSpec(memory_space=pltpu.VMEM)] * PLANE + [pl.BlockSpec(memory_space=pl.ANY)],
        out_specs=[pl.BlockSpec(memory_space=pltpu.VMEM)] * lines,
        compiler_params=pltpu.CompilerParams(vmem_limit_bytes=VMEM),
        cost_estimate=SMALL,
    )(*parts, after)


def gather_window(parts, cores, pairs, after):
    lines = len(parts)
    rows, offsets = parts[0].shape
    group = lines * pairs
    taken = PLANE * group

    def kernel(*refs):
        total = 0.0
        for s in range(lines):

            def source(row):
                h, r, at, p = row // taken, row % taken // group, row % group // pairs, row % pairs
                return jnp.where(at == s, (h * PLANE + r) * pairs + p, -1)

            total += jnp.dot(select(cores * taken, rows, source), refs[s][...], preferred_element_type=F32)
        for h in range(cores):
            refs[-1][:, pl.ds(h * offsets, offsets)] = total[h * taken : (h + 1) * taken].astype(BF16)

    return pl.pallas_call(
        kernel,
        out_shape=jax.ShapeDtypeStruct((taken, cores * offsets), BF16),
        in_specs=[pl.BlockSpec(memory_space=pltpu.VMEM)] * lines + [pl.BlockSpec(memory_space=pl.ANY)],
        out_specs=pl.BlockSpec(memory_space=pltpu.VMEM),
        compiler_params=pltpu.CompilerParams(vmem_limit_bytes=VMEM),
        cost_estimate=SMALL,
    )(*parts, after)


def multiply(window_ref, chunk_ref, at, tile):
    rows, depth = window_ref.shape
    half = tile // 2
    if half != MATRIX or depth % MATRIX or rows % 16:
        return jnp.dot(window_ref[...], chunk_ref[:, pl.ds(at, tile)], preferred_element_type=F32)

    def body(*sums):
        for k in range(depth // MATRIX):
            ks = pl.ds(k * MATRIX, MATRIX)
            for unit in range(2):
                pltpu.matmul_push_rhs(chunk_ref[ks, pl.ds(at + unit * half, half)], k % 2, unit)
            for unit in range(2):
                pltpu.matmul_acc_lhs(sums[unit], window_ref[:, ks], k % 2)
        return jnp.concatenate([pltpu.matmul_pop(sums[unit]) for unit in range(2)], axis=1)

    return pl.run_scoped(body, pltpu.ACC(0)((rows, half), F32), pltpu.ACC(1)((rows, half), F32))


def product(window, integral, ready, start, stream, more, unit, after):
    group = window.shape[0] // PLANE
    depth = integral.shape[0]
    parts = fold(group)
    columns = sum(chunk.shape[1] for chunk in ready) + stream
    width = columns // parts
    tile = next(t for t in (TILE, 256, 128) if unit % t == 0)
    steps = stream // unit

    def kernel(window_ref, integral_ref, *refs):
        chunks, refs = refs[: len(ready)], refs[len(ready) + len(after) :]
        own, outs, refs = refs[0], refs[1:PLANE], refs[PLANE:]
        kept, ring, sems, more_sems = refs[-4:]
        incoming = [
            copies(integral_ref, start + k * unit, unit, ring.at[k % SLOTS], sems.at[k % SLOTS]) for k in range(steps)
        ]
        handed = [
            copies(integral_ref, start + stream + k * unit, unit, refs[0].at[:, pl.ds(k * unit, unit)], more_sems.at[k])
            for k in range(more // unit)
        ]
        for move in sum(incoming[: SLOTS - 1], []):
            move.start()

        def tiles(chunk_ref, column, largest):
            part, offset = divmod(column, width)

            def step(i, largest):
                at = pl.multiple_of(i * tile, tile)
                sums = multiply(window_ref, chunk_ref, at, tile)
                at = pl.ds(offset + at, tile)
                for begin, rows, where in packed_rows(group, part):
                    own[where : where + rows, at] = sums[begin : begin + rows]
                    for r in range(1, PLANE):
                        kept[r - 1, where : where + rows, at] = sums[r * group + begin : r * group + begin + rows]
                return jnp.maximum(largest, jnp.abs(sums[group:]))

            return lax.fori_loop(0, unit // tile, step, largest)

        held = [
            chunk_ref.at[:, pl.ds(at, unit)] for chunk_ref in chunks for at in range(0, chunk_ref.shape[1], unit)
        ]
        largest = jnp.zeros(((PLANE - 1) * group, tile), F32)
        for k in range(max(len(held), steps)):
            if k < len(held):
                largest = tiles(held[k], k * unit, largest)
            if k < steps:
                for move in incoming[k]:
                    move.wait()
                for move in incoming[k + SLOTS - 1] if k + SLOTS - 1 < steps else []:
                    move.start()
                largest = tiles(ring.at[k % SLOTS], (len(held) + k) * unit, largest)
            if k % 3 == 2 and k // 3 < len(handed):
                for move in handed[k // 3]:
                    move.start()

        largest = jnp.max(largest, keepdims=True)
        for r, out in enumerate(outs):

            @pl.loop(0, width // tile)
            def _(i):
                at = pl.ds(pl.multiple_of(i * tile, tile), tile)
                out[:, at] = encode(kept[r, :, at], largest)[0]

            out[:, pl.ds(width, LANES)] = jnp.broadcast_to(encode(largest, largest)[1], (parts * group, LANES))
        for move in sum(handed, []):
            move.wait()

    shapes = [pltpu.VMEM((parts * group, width), F32)]
    shapes += [pltpu.VMEM((parts * group, width + LANES), BF16)] * (PLANE - 1)
    if more:
        shapes.append(pltpu.VMEM((depth, more), BF16))
    ready = [pltpu.with_memory_space_constraint(chunk, pltpu.VMEM) for chunk in ready]
    return pl.pallas_call(
        kernel,
        out_shape=shapes,
        in_specs=[pl.BlockSpec(memory_space=pltpu.VMEM), pl.BlockSpec(memory_space=pl.ANY)]
        + [pl.BlockSpec(memory_space=pltpu.VMEM)] * len(ready)
        + [pl.BlockSpec(memory_space=pl.ANY)] * len(after),
        out_specs=[pl.BlockSpec(memory_space=pltpu.VMEM)] * len(shapes),
        scratch_shapes=[
            pltpu.VMEM((PLANE - 1, parts * group, width), F32),
            pltpu.VMEM((min(SLOTS, steps), depth, unit), BF16),
            pltpu.SemaphoreType.DMA((min(SLOTS, steps), PIECES)),
            pltpu.SemaphoreType.DMA((max(more // unit, 1), PIECES)),
        ],
        compiler_params=pltpu.CompilerParams(vmem_limit_bytes=VMEM),
        cost_estimate=pl.CostEstimate(
            flops=2 * window.shape[0] * depth * columns, bytes_accessed=depth * columns * 2, transcendentals=0
        ),
    )(window, integral, *ready, *after)


def line_fold(width, parts):
    return next(n for n in (8, 4, 2, 1) if n * parts <= 8 and width % (n * LANES) == 0)


def add_plane(chunk, lines, pairs):
    group = lines * pairs
    parts = fold(group)
    width = chunk[0].shape[1]
    pieces = line_fold(width, parts)
    rows, columns = parts * pieces * pairs, width // pieces

    def kernel(*refs):
        ins, own, outs, kept = refs[:PLANE], refs[PLANE], refs[PLANE + 1 : -1], refs[-1]
        total = ins[0][...]
        for ref in ins[1:]:
            total += decode(ref[:, pl.ds(0, width)], ref[:, pl.ds(width, 1)])
        for s in range(lines):
            for j, part in enumerate(unpacked(total, group, s * pairs, pairs)):
                for k in range(pieces):
                    row = pl.ds((j * pieces + k) * pairs, pairs)
                    value = part[:, k * columns : (k + 1) * columns]
                    if s == 0:
                        own[row, :] = value
                    else:
                        kept[s - 1, row, :] = value
        largest = jnp.max(jnp.abs(total), keepdims=True)
        for s, out in enumerate(outs):
            code, scale = encode(kept[s], largest)
            out[:, pl.ds(0, columns)] = code
            out[:, pl.ds(columns, LANES)] = jnp.broadcast_to(scale, (rows, LANES))

    code = jax.ShapeDtypeStruct((rows, columns + LANES), BF16)
    return pl.pallas_call(
        kernel,
        out_shape=[jax.ShapeDtypeStruct((rows, columns), F32)] + [code] * (lines - 1),
        in_specs=[pl.BlockSpec(memory_space=pltpu.VMEM)] * PLANE,
        out_specs=[pl.BlockSpec(memory_space=pltpu.VMEM)] * lines,
        scratch_shapes=[pltpu.VMEM((lines - 1, rows, columns), F32)],
        compiler_params=pltpu.CompilerParams(vmem_limit_bytes=VMEM),
        cost_estimate=SMALL,
    )(*chunk)


def add_line(own, codes, before, pairs):
    columns = own.shape[1]

    def kernel(own_ref, *refs):
        out = refs[-1]
        total = own_ref[...]
        for ref in refs[: len(codes)]:
            total += decode(ref[:, pl.ds(0, columns)], ref[:, pl.ds(columns, 1)])
        if not before:
            out[...] = total
            return
        start = 0
        for array in [ref[...] for ref in refs[len(codes) : -1]] + [total]:
            for j in range(array.shape[0] // pairs):
                out[:, pl.ds(start, array.shape[1])] = array[j * pairs : (j + 1) * pairs]
                start += array.shape[1]

    size = sum(array.size for array in [*before, own])
    return pl.pallas_call(
        kernel,
        out_shape=jax.ShapeDtypeStruct((pairs, size // pairs) if before else own.shape, F32),
        in_specs=[pl.BlockSpec(memory_space=pltpu.VMEM)] * (1 + len(codes) + len(before)),
        out_specs=pl.BlockSpec(memory_space=pltpu.VMEM),
        compiler_params=pltpu.CompilerParams(vmem_limit_bytes=VMEM),
        cost_estimate=SMALL,
    )(own, *codes, *before)


def per_device(owners, cores, amplitudes, integral):
    pairs = amplitudes.shape[0]
    lines = owners // PLANE
    def swap(axis, size, array, by):
        return lax.ppermute(array, axis, [(i, i ^ by) for i in range(size)])

    plane = functools.partial(swap, "ab", owners)
    line = lambda array, by: swap("ab", owners, array, by * PLANE)
    core = functools.partial(swap, "cd", cores)

    unit = integral.shape[1] // UNITS
    early, late = (count * unit for count in AHEAD)

    halves = [amplitudes] + [core(amplitudes, j) for j in range(1, cores)]
    parts = split_by_plane(halves, lines)
    ready = [load(0, early, unit, integral, parts[0])]
    parts = [parts[0]] + [plane(parts[r], r) for r in range(1, PLANE)]
    parts = split_by_line(parts, cores, lines, pairs, ready[-1])
    ready.append(load(early, late, unit, integral, parts[0]))
    parts = [parts[0]] + [line(parts[s], s) for s in range(1, lines)]
    window = gather_window(parts, cores, pairs, ready[-1])

    start, more = early + late, MORE * unit
    own, *codes, chunk = product(window, integral, ready, start, STREAM * unit, more, unit, [])
    chunks = [[own] + [plane(code, r + 1) for r, code in enumerate(codes)]]
    start += STREAM * unit + more
    own, *codes = product(window, integral, [chunk], start, SECOND * unit - more, 0, unit, [own])
    chunks.append([own] + [plane(code, r + 1) for r, code in enumerate(codes)])
    sums = []
    for chunk in chunks:
        own, *codes = add_plane(chunk, lines, pairs)
        sums.append(add_line(own, [line(code, s + 1) for s, code in enumerate(codes)], sums, pairs))
    return sums[-1]


def solution(mesh):
    placed = (P("ab", None, "cd"), P("ab", "cd"))
    return jax.shard_map(
        functools.partial(per_device, mesh.shape["ab"], mesh.shape["cd"]),
        mesh=mesh,
        in_specs=placed,
        out_specs=P("ab", "cd"),
        check_vma=False,
    )
```

time: 186 us -> 64.3 us (0.35)
  waiting for transfers between devices: 121 us -> 8.83 us
  Pallas kernels: 0 us -> 28.9 us
  starting transfers between devices: 0.01 us -> 25.4 us
  matrix products: 24.2 us -> 0 us
  blocking collectives: 23.1 us -> 0 us
  between operations: 14.1 us -> 0.13 us
  local copies, waits for them, and re-layouts: 3.67 us -> 0.91 us
    unnamed x2 -> x0, waiting for transfers between devices: 121 us -> none
    pallas_call x0 -> x11, Pallas kernels: none -> 28.9 us  [the longest x2 16.9 us: product(): pl.pallas_call(kernel, out_shape=shapes, in_specs=[pl.BlockSpec(memory_sp...]
    ppermute x0 -> x19, starting transfers between devices: none -> 25.4 us  [swap(): return lax.ppermute(array, axis, [(i, i ^ by) for i in range(size)])]
    dot_general x1 -> x0, matrix products: 24.2 us -> none  [per_device(): jnp.dot(window, integral, preferred_element_type=jnp.float32)]
    all_to_all x1 -> x0, blocking collectives: 20.9 us -> none  [per_device(): lax.all_to_all(widened, 'ab', split_axis=1, concat_axis=0, tiled=True)]
    ppermute x0 -> x19, waiting for transfers between devices: none -> 8.83 us  [swap(): return lax.ppermute(array, axis, [(i, i ^ by) for i in range(size)])]
    unnamed x5 -> x2, local copies, waits for them, and re-layouts: 3.43 us -> 0.91 us
    all_gather x1 -> x0, blocking collectives: 2.17 us -> none  [per_device(): widened = lax.all_gather(amplitudes, 'cd', axis=2, tiled=True)]
  transfers between devices with their start and end apart: 1 -> 19, of which waited for: 1 -> 6; matrix products, arithmetic and copies ran while one was open for 0% -> 0% of each run, Pallas kernels for 0% -> 25%
where the time goes in v1:
time: 64.3 us; the launch traced here: 64.1 us
  Pallas kernels  28.9 us (45%)
  starting transfers between devices  25.4 us (40%)
  waiting for transfers between devices  8.83 us (14%)
  local copies, waits for them, and re-layouts  0.91 us (1%)
    ppermute x19, starting transfers between devices, swap(): return lax.ppermute(array, axis, [(i, i ^ by) for i in range(size)])  25.4 us
    pallas_call x2, Pallas kernels, product(): pl.pallas_call(kernel, out_shape=shapes, in_specs=[pl.BlockSpec(memory_sp...  16.9 us
    ppermute x19, waiting for transfers between devices, swap(): return lax.ppermute(array, axis, [(i, i ^ by) for i in range(size)])  8.83 us
    pallas_call x2, Pallas kernels, load(): pl.pallas_call(kernel, out_shape=pltpu.VMEM((depth, columns), BF16), in_s...  8.67 us
  transfers between devices with their start and end apart: 19, of which 6 were waited for; matrix products, arithmetic and copies ran while one was open for 0% of the time, Pallas kernels for 25%

profile of v1, /device:TPU:0, one launch (start us, length us, event | category | flops | bytes accessed | tf_op | source)
XLA Modules:
  0.0 64.1 jit_solution(1297551040719418421)
XLA Ops:
  0.0 0.5 collective-permute-start
  0.5 1.2 %collective-permute-done.refs_1_ = bf16[3,16,1536]{2,1,0:T(8,128)(2,1)S(1)} collective-permute-done((bf16[3,16,1536]{2,1,0:T(8,128)(2,1)}, bf16[3,16,1536]{2,1,0:T(8,128)(2,1)S(1)}, u32[]{:S(2)}, u32[]{:S(2)}) %collective-permute-start) | collective-permute-done | bytes 147488 | tf_op jit(solution)/shard_map/ppermute | solution.py:382
  1.7 0.9 %copy-done = bf16[3,16,1536]{2,1,0:T(8,128)(2,1)S(1)} copy-done((bf16[3,16,1536]{2,1,0:T(8,128)(2,1)S(1)}, bf16[3,16,1536]{2,1,0:T(8,128)(2,1)}, u32[]{:S(2)}) %copy-start) | copy-done | bytes 147480
  2.6 0.4 shard_map.28
  3.0 2.9 %collective-permute-start.1 = (bf16[24,1536]{1,0:T(8,128)(2,1)S(1)}, bf16[24,1536]{1,0:T(8,128)(2,1)S(1)}, u32[]{:S(2)}, u32[]{:S(2)}) collective-permute-start(bf16[24,1536]{1,0:T(8,128)(2,1)S(1)} %get-tuple-element.31), channel_id=1, source_target_pairs={{0,2},{2,0},{4,6},{6,4},{8,10},{10,8},{12,14},{14,12},{16,18},{18,... | collective-permute-start | bytes 221192 | tf_op jit(solution)/shard_map/ppermute | solution.py:382
  5.9 1.5 %collective-permute-start.2 = (bf16[24,1536]{1,0:T(8,128)(2,1)S(1)}, bf16[24,1536]{1,0:T(8,128)(2,1)S(1)}, u32[]{:S(2)}, u32[]{:S(2)}) collective-permute-start(bf16[24,1536]{1,0:T(8,128)(2,1)S(1)} %get-tuple-element.32), channel_id=1, source_target_pairs={{0,4},{2,6},{4,0},{6,2},{8,12},{10,14},{12,8},{14,10},{16,20},{18,... | collective-permute-start | bytes 221192 | tf_op jit(solution)/shard_map/ppermute | solution.py:382
  7.4 2.9 %shard_map.29.refs_4_.refs_0_ = bf16[3072,1024]{1,0:T(8,128)(2,1)S(1)} custom-call(bf16[3072,10240]{1,0:T(8,128)(2,1)} %integral_ref.7, bf16[24,1536]{1,0:T(8,128)(2,1)S(1)} %get-tuple-element.30.after_ref.refs_0_), custom_call_target="tpu_custom_call" | custom-call | bytes 6291456 | tf_op jit(solution)/shard_map/pallas_call | solution.py:59
  10.4 2.3 %collective-permute-done.3.refs_3_ = bf16[24,1536]{1,0:T(8,128)(2,1)S(1)} collective-permute-done((bf16[24,1536]{1,0:T(8,128)(2,1)S(1)}, bf16[24,1536]{1,0:T(8,128)(2,1)S(1)}, u32[]{:S(2)}, u32[]{:S(2)}) %collective-permute-start.3) | collective-permute-done | bytes 73760 | tf_op jit(solution)/shard_map/ppermute | solution.py:382
  12.7 0.5 shard_map.30
  13.2 1.6 %collective-permute-start.4 = (bf16[24,1536]{1,0:T(8,128)(2,1)S(1)}, bf16[24,1536]{1,0:T(8,128)(2,1)S(1)}, u32[]{:S(2)}, u32[]{:S(2)}) collective-permute-start(bf16[24,1536]{1,0:T(8,128)(2,1)S(1)} %get-tuple-element.35), channel_id=1, source_target_pairs={{0,8},{2,10},{4,12},{6,14},{8,0},{10,2},{12,4},{14,6},{16,24},{18,... | collective-permute-start | bytes 221192 | tf_op jit(solution)/shard_map/ppermute | solution.py:382
  14.8 2.6 %collective-permute-start.5 = (bf16[24,1536]{1,0:T(8,128)(2,1)S(1)}, bf16[24,1536]{1,0:T(8,128)(2,1)S(1)}, u32[]{:S(2)}, u32[]{:S(2)}) collective-permute-start(bf16[24,1536]{1,0:T(8,128)(2,1)S(1)} %get-tuple-element.36), channel_id=1, source_target_pairs={{0,16},{2,18},{4,20},{6,22},{8,24},{10,26},{12,28},{14,30},{16,0},... | collective-permute-start | bytes 221192 | tf_op jit(solution)/shard_map/ppermute | solution.py:382
  17.6 5.8 %shard_map.31.refs_4_.refs_1_ = bf16[3072,2560]{1,0:T(8,128)(2,1)S(1)} custom-call(bf16[3072,10240]{1,0:T(8,128)(2,1)} %integral_ref.7, bf16[24,1536]{1,0:T(8,128)(2,1)S(1)} %get-tuple-element.34.after_ref.refs_0_), custom_call_target="tpu_custom_call" | custom-call | bytes 15728640 | tf_op jit(solution)/shard_map/pallas_call | solution.py:59
  23.6 0.5 shard_map.32.window_ref
  24.1 10.8 %shard_map.33 = (f32[24,3584]{1,0:T(8,128)S(1)}, bf16[24,3712]{1,0:T(8,128)(2,1)S(1)}, bf16[24,3712]{1,0:T(8,128)(2,1)S(1)}, bf16[24,3712]{1,0:T(8,128)(2,1)S(1)}, bf16[3072,1024]{1,0:T(8,128)(2,1)S(1)}) custom-call(bf16[48,3072]{1,0:T(8,128)(2,1)S(1)} %shard_map.32.window_ref, bf16[3072,10240]{1,0:T(8,128)(2,1)} %integral_ref.7, ...), custom_call_target="tpu_custom_call" | custom-call | flops 2113929216 | bytes 44040192 | tf_op jit(solution)/shard_map/pallas_call | solution.py:287
  34.9 0.6 collective-permute-start.13
  35.5 0.7 %collective-permute-start.14 = (bf16[24,3712]{1,0:T(8,128)(2,1)S(1)}, bf16[24,3712]{1,0:T(8,128)(2,1)S(1)}, u32[]{:S(2)}, u32[]{:S(2)}) collective-permute-start(bf16[24,3712]{1,0:T(8,128)(2,1)S(1)} %get-tuple-element.49), channel_id=1, source_target_pairs={{0,4},{2,6},{4,0},{6,2},{8,12},{10,14},{12,8},{14,10},{16,20},{18,... | collective-permute-start | bytes 534536 | tf_op jit(solution)/shard_map/ppermute | solution.py:382
  36.3 2.2 %collective-permute-start.15 = (bf16[24,3712]{1,0:T(8,128)(2,1)S(1)}, bf16[24,3712]{1,0:T(8,128)(2,1)S(1)}, u32[]{:S(2)}, u32[]{:S(2)}) collective-permute-start(bf16[24,3712]{1,0:T(8,128)(2,1)S(1)} %get-tuple-element.50), channel_id=1, source_target_pairs={{0,6},{2,4},{4,2},{6,0},{8,14},{10,12},{12,10},{14,8},{16,22},{18,... | collective-permute-start | bytes 534536 | tf_op jit(solution)/shard_map/ppermute | solution.py:382
  38.5 6.1 %shard_map.34 = (f32[24,1536]{1,0:T(8,128)S(1)}, bf16[24,1664]{1,0:T(8,128)(2,1)S(1)}, bf16[24,1664]{1,0:T(8,128)(2,1)S(1)}, bf16[24,1664]{1,0:T(8,128)(2,1)S(1)}) custom-call(bf16[48,3072]{1,0:T(8,128)(2,1)S(1)} %shard_map.32.window_ref, bf16[3072,10240]{1,0:T(8,128)(2,1)} %integral_ref.7, bf16[3072,1024]{1,0:T(8,128)(2,1)S(1)} %get-tuple-element.38.refs_0_, ...), custom_call_target="tpu_custom_call" | custom-call | flops 905969664 | bytes 18874368 | tf_op jit(solution)/shard_map/pallas_call | solution.py:287
  44.5 0.6 collective-permute-start.7
  45.1 0.7 %collective-permute-start.8 = (bf16[24,1664]{1,0:T(8,128)(2,1)S(1)}, bf16[24,1664]{1,0:T(8,128)(2,1)S(1)}, u32[]{:S(2)}, u32[]{:S(2)}) collective-permute-start(bf16[24,1664]{1,0:T(8,128)(2,1)S(1)} %get-tuple-element.42), channel_id=1, source_target_pairs={{0,4},{2,6},{4,0},{6,2},{8,12},{10,14},{12,8},{14,10},{16,20},{18,... | collective-permute-start | bytes 239624 | tf_op jit(solution)/shard_map/ppermute | solution.py:382
  45.9 2.2 %collective-permute-start.9 = (bf16[24,1664]{1,0:T(8,128)(2,1)S(1)}, bf16[24,1664]{1,0:T(8,128)(2,1)S(1)}, u32[]{:S(2)}, u32[]{:S(2)}) collective-permute-start(bf16[24,1664]{1,0:T(8,128)(2,1)S(1)} %get-tuple-element.43), channel_id=1, source_target_pairs={{0,6},{2,4},{4,2},{6,0},{8,14},{10,12},{12,10},{14,8},{16,22},{18,... | collective-permute-start | bytes 239624 | tf_op jit(solution)/shard_map/ppermute | solution.py:382
  48.1 0.7 %shard_map.36 = (f32[24,896]{1,0:T(8,128)S(1)}, bf16[24,1024]{1,0:T(8,128)(2,1)S(1)}, bf16[24,1024]{1,0:T(8,128)(2,1)S(1)}, bf16[24,1024]{1,0:T(8,128)(2,1)S(1)}) custom-call(f32[24,3584]{1,0:T(8,128)S(1)} %get-tuple-element.39.refs_1_.refs_0_, bf16[24,3712]{1,0:T(8,128)(2,1)S(1)} %collective-permute-done.13.refs_1_, ...), custom_call_target="tpu_custom_call" | custom-call | flops 1048576 | bytes 1048576 | tf_op jit(solution)/shard_map/pallas_call | solution.py:339
  48.8 0.6 collective-permute-start.16
  49.4 3.5 %collective-permute-start.17 = (bf16[24,1024]{1,0:T(8,128)(2,1)S(1)}, bf16[24,1024]{1,0:T(8,128)(2,1)S(1)}, u32[]{:S(2)}, u32[]{:S(2)}) collective-permute-start(bf16[24,1024]{1,0:T(8,128)(2,1)S(1)} %get-tuple-element.53), channel_id=1, source_target_pairs={{0,16},{2,18},{4,20},{6,22},{8,24},{10,26},{12,28},{14,30},{16,0},... | collective-permute-start | bytes 147464 | tf_op jit(solution)/shard_map/ppermute | solution.py:382
  52.9 0.3 collective-permute-start.18
  53.2 0.4 shard_map.35
  53.9 3.8 %collective-permute-start.11 = (bf16[24,512]{1,0:T(8,128)(2,1)S(1)}, bf16[24,512]{1,0:T(8,128)(2,1)S(1)}, u32[]{:S(2)}, u32[]{:S(2)}) collective-permute-start(bf16[24,512]{1,0:T(8,128)(2,1)S(1)} %get-tuple-element.46), channel_id=1, source_target_pairs={{0,16},{2,18},{4,20},{6,22},{8,24},{10,26},{12,28},{14,30},{16,0},... | collective-permute-start | bytes 73736 | tf_op jit(solution)/shard_map/ppermute | solution.py:382
  57.7 0.3 collective-permute-start.12
  58.1 0.7 %collective-permute-done.18.refs_2_ = bf16[24,1024]{1,0:T(8,128)(2,1)S(1)} collective-permute-done((bf16[24,1024]{1,0:T(8,128)(2,1)S(1)}, bf16[24,1024]{1,0:T(8,128)(2,1)S(1)}, u32[]{:S(2)}, u32[]{:S(2)}) %collective-permute-start.18) | collective-permute-done | bytes 49184 | tf_op jit(solution)/shard_map/ppermute | solution.py:382
  58.9 0.6 collective-permute-done.11.refs_1_
  59.5 3.8 %collective-permute-done.12.refs_2_ = bf16[24,512]{1,0:T(8,128)(2,1)S(1)} collective-permute-done((bf16[24,512]{1,0:T(8,128)(2,1)S(1)}, bf16[24,512]{1,0:T(8,128)(2,1)S(1)}, u32[]{:S(2)}, u32[]{:S(2)}) %collective-permute-start.12) | collective-permute-done | bytes 24608 | tf_op jit(solution)/shard_map/ppermute | solution.py:382
  63.4 0.8 %shard_map.38 = f32[3,10240]{1,0:T(4,128)} custom-call(f32[24,384]{1,0:T(8,128)S(1)} %get-tuple-element.44.own_ref, bf16[24,512]{1,0:T(8,128)(2,1)S(1)} %collective-permute-done.10.refs_0_, bf16[24,512]{1,0:T(8,128)(2,1)S(1)} %collective-permute-done.11.refs_1_, bf16[24,512]{1,0:T(8,128)(2,1)S(1)} %collective-permute-done.12.refs_2_, ...), custom_call_target="tpu_custom_call" | custom-call | flops 1048576 | bytes 1048576 | tf_op jit(solution)/shard_map/pallas_call | solution.py:368
  (19 shorter events, 0.8 us)
Async XLA Ops:
  0.0 1.7 %collective-permute-start = (bf16[3,16,1536]{2,1,0:T(8,128)(2,1)}, bf16[3,16,1536]{2,1,0:T(8,128)(2,1)S(1)}, u32[]{:S(2)}, u32[]{:S(2)}) collective-permute-start(bf16[3,16,1536]{2,1,0:T(8,128)(2,1)} %refs_0_.1), channel_id=1, source_target_pairs={{0,1},{1,0},{2,3},{3,2},{4,5},{5,4},{6,7},{7,6},{8,9},{9,8},{10,11... | collective-permute-start | bytes 442376 | tf_op jit(solution)/shard_map/ppermute | solution.py:382
  1.7 0.9 %copy-start = (bf16[3,16,1536]{2,1,0:T(8,128)(2,1)S(1)}, bf16[3,16,1536]{2,1,0:T(8,128)(2,1)}, u32[]{:S(2)}) copy-start(bf16[3,16,1536]{2,1,0:T(8,128)(2,1)} %refs_0_.1) | copy-start | bytes 442372
  3.0 7.4 %collective-permute-start.1 = (bf16[24,1536]{1,0:T(8,128)(2,1)S(1)}, bf16[24,1536]{1,0:T(8,128)(2,1)S(1)}, u32[]{:S(2)}, u32[]{:S(2)}) collective-permute-start(bf16[24,1536]{1,0:T(8,128)(2,1)S(1)} %get-tuple-element.31), channel_id=1, source_target_pairs={{0,2},{2,0},{4,6},{6,4},{8,10},{10,8},{12,14},{14,12},{16,18},{18,... | collective-permute-start | bytes 221192 | tf_op jit(solution)/shard_map/ppermute | solution.py:382
  5.9 4.5 %collective-permute-start.2 = (bf16[24,1536]{1,0:T(8,128)(2,1)S(1)}, bf16[24,1536]{1,0:T(8,128)(2,1)S(1)}, u32[]{:S(2)}, u32[]{:S(2)}) collective-permute-start(bf16[24,1536]{1,0:T(8,128)(2,1)S(1)} %get-tuple-element.32), channel_id=1, source_target_pairs={{0,4},{2,6},{4,0},{6,2},{8,12},{10,14},{12,8},{14,10},{16,20},{18,... | collective-permute-start | bytes 221192 | tf_op jit(solution)/shard_map/ppermute | solution.py:382
  7.4 5.3 %collective-permute-start.3 = (bf16[24,1536]{1,0:T(8,128)(2,1)S(1)}, bf16[24,1536]{1,0:T(8,128)(2,1)S(1)}, u32[]{:S(2)}, u32[]{:S(2)}) collective-permute-start(bf16[24,1536]{1,0:T(8,128)(2,1)S(1)} %get-tuple-element.33), channel_id=1, source_target_pairs={{0,6},{2,4},{4,2},{6,0},{8,14},{10,12},{12,10},{14,8},{16,22},{18,... | collective-permute-start | bytes 221192 | tf_op jit(solution)/shard_map/ppermute | solution.py:382
  13.2 10.2 %collective-permute-start.4 = (bf16[24,1536]{1,0:T(8,128)(2,1)S(1)}, bf16[24,1536]{1,0:T(8,128)(2,1)S(1)}, u32[]{:S(2)}, u32[]{:S(2)}) collective-permute-start(bf16[24,1536]{1,0:T(8,128)(2,1)S(1)} %get-tuple-element.35), channel_id=1, source_target_pairs={{0,8},{2,10},{4,12},{6,14},{8,0},{10,2},{12,4},{14,6},{16,24},{18,... | collective-permute-start | bytes 221192 | tf_op jit(solution)/shard_map/ppermute | solution.py:382
  14.8 8.6 %collective-permute-start.5 = (bf16[24,1536]{1,0:T(8,128)(2,1)S(1)}, bf16[24,1536]{1,0:T(8,128)(2,1)S(1)}, u32[]{:S(2)}, u32[]{:S(2)}) collective-permute-start(bf16[24,1536]{1,0:T(8,128)(2,1)S(1)} %get-tuple-element.36), channel_id=1, source_target_pairs={{0,16},{2,18},{4,20},{6,22},{8,24},{10,26},{12,28},{14,30},{16,0},... | collective-permute-start | bytes 221192 | tf_op jit(solution)/shard_map/ppermute | solution.py:382
  17.4 6.2 %collective-permute-start.6 = (bf16[24,1536]{1,0:T(8,128)(2,1)S(1)}, bf16[24,1536]{1,0:T(8,128)(2,1)S(1)}, u32[]{:S(2)}, u32[]{:S(2)}) collective-permute-start(bf16[24,1536]{1,0:T(8,128)(2,1)S(1)} %get-tuple-element.37), channel_id=1, source_target_pairs={{0,24},{2,26},{4,28},{6,30},{8,16},{10,18},{12,20},{14,22},{16,8},... | collective-permute-start | bytes 221192 | tf_op jit(solution)/shard_map/ppermute | solution.py:382
  34.9 11.0 %collective-permute-start.13 = (bf16[24,3712]{1,0:T(8,128)(2,1)S(1)}, bf16[24,3712]{1,0:T(8,128)(2,1)S(1)}, u32[]{:S(2)}, u32[]{:S(2)}) collective-permute-start(bf16[24,3712]{1,0:T(8,128)(2,1)S(1)} %get-tuple-element.48), channel_id=1, source_target_pairs={{0,2},{2,0},{4,6},{6,4},{8,10},{10,8},{12,14},{14,12},{16,18},{18,... | collective-permute-start | bytes 534536 | tf_op jit(solution)/shard_map/ppermute | solution.py:382
  35.5 12.6 %collective-permute-start.14 = (bf16[24,3712]{1,0:T(8,128)(2,1)S(1)}, bf16[24,3712]{1,0:T(8,128)(2,1)S(1)}, u32[]{:S(2)}, u32[]{:S(2)}) collective-permute-start(bf16[24,3712]{1,0:T(8,128)(2,1)S(1)} %get-tuple-element.49), channel_id=1, source_target_pairs={{0,4},{2,6},{4,0},{6,2},{8,12},{10,14},{12,8},{14,10},{16,20},{18,... | collective-permute-start | bytes 534536 | tf_op jit(solution)/shard_map/ppermute | solution.py:382
  36.3 11.8 %collective-permute-start.15 = (bf16[24,3712]{1,0:T(8,128)(2,1)S(1)}, bf16[24,3712]{1,0:T(8,128)(2,1)S(1)}, u32[]{:S(2)}, u32[]{:S(2)}) collective-permute-start(bf16[24,3712]{1,0:T(8,128)(2,1)S(1)} %get-tuple-element.50), channel_id=1, source_target_pairs={{0,6},{2,4},{4,2},{6,0},{8,14},{10,12},{12,10},{14,8},{16,22},{18,... | collective-permute-start | bytes 534536 | tf_op jit(solution)/shard_map/ppermute | solution.py:382
  44.5 8.3 %collective-permute-start.7 = (bf16[24,1664]{1,0:T(8,128)(2,1)S(1)}, bf16[24,1664]{1,0:T(8,128)(2,1)S(1)}, u32[]{:S(2)}, u32[]{:S(2)}) collective-permute-start(bf16[24,1664]{1,0:T(8,128)(2,1)S(1)} %get-tuple-element.41), channel_id=1, source_target_pairs={{0,2},{2,0},{4,6},{6,4},{8,10},{10,8},{12,14},{14,12},{16,18},{18,... | collective-permute-start | bytes 239624 | tf_op jit(solution)/shard_map/ppermute | solution.py:382
  45.1 8.1 %collective-permute-start.8 = (bf16[24,1664]{1,0:T(8,128)(2,1)S(1)}, bf16[24,1664]{1,0:T(8,128)(2,1)S(1)}, u32[]{:S(2)}, u32[]{:S(2)}) collective-permute-start(bf16[24,1664]{1,0:T(8,128)(2,1)S(1)} %get-tuple-element.42), channel_id=1, source_target_pairs={{0,4},{2,6},{4,0},{6,2},{8,12},{10,14},{12,8},{14,10},{16,20},{18,... | collective-permute-start | bytes 239624 | tf_op jit(solution)/shard_map/ppermute | solution.py:382
  45.9 7.3 %collective-permute-start.9 = (bf16[24,1664]{1,0:T(8,128)(2,1)S(1)}, bf16[24,1664]{1,0:T(8,128)(2,1)S(1)}, u32[]{:S(2)}, u32[]{:S(2)}) collective-permute-start(bf16[24,1664]{1,0:T(8,128)(2,1)S(1)} %get-tuple-element.43), channel_id=1, source_target_pairs={{0,6},{2,4},{4,2},{6,0},{8,14},{10,12},{12,10},{14,8},{16,22},{18,... | collective-permute-start | bytes 239624 | tf_op jit(solution)/shard_map/ppermute | solution.py:382
  48.8 9.0 %collective-permute-start.16 = (bf16[24,1024]{1,0:T(8,128)(2,1)S(1)}, bf16[24,1024]{1,0:T(8,128)(2,1)S(1)}, u32[]{:S(2)}, u32[]{:S(2)}) collective-permute-start(bf16[24,1024]{1,0:T(8,128)(2,1)S(1)} %get-tuple-element.52), channel_id=1, source_target_pairs={{0,8},{2,10},{4,12},{6,14},{8,0},{10,2},{12,4},{14,6},{16,24},{18,... | collective-permute-start | bytes 147464 | tf_op jit(solution)/shard_map/ppermute | solution.py:382
  49.4 8.7 %collective-permute-start.17 = (bf16[24,1024]{1,0:T(8,128)(2,1)S(1)}, bf16[24,1024]{1,0:T(8,128)(2,1)S(1)}, u32[]{:S(2)}, u32[]{:S(2)}) collective-permute-start(bf16[24,1024]{1,0:T(8,128)(2,1)S(1)} %get-tuple-element.53), channel_id=1, source_target_pairs={{0,16},{2,18},{4,20},{6,22},{8,24},{10,26},{12,28},{14,30},{16,0},... | collective-permute-start | bytes 147464 | tf_op jit(solution)/shard_map/ppermute | solution.py:382
  52.9 5.9 %collective-permute-start.18 = (bf16[24,1024]{1,0:T(8,128)(2,1)S(1)}, bf16[24,1024]{1,0:T(8,128)(2,1)S(1)}, u32[]{:S(2)}, u32[]{:S(2)}) collective-permute-start(bf16[24,1024]{1,0:T(8,128)(2,1)S(1)} %get-tuple-element.54), channel_id=1, source_target_pairs={{0,24},{2,26},{4,28},{6,30},{8,16},{10,18},{12,20},{14,22},{16,8},... | collective-permute-start | bytes 147464 | tf_op jit(solution)/shard_map/ppermute | solution.py:382
  53.6 5.3 %collective-permute-start.10 = (bf16[24,512]{1,0:T(8,128)(2,1)S(1)}, bf16[24,512]{1,0:T(8,128)(2,1)S(1)}, u32[]{:S(2)}, u32[]{:S(2)}) collective-permute-start(bf16[24,512]{1,0:T(8,128)(2,1)S(1)} %get-tuple-element.45), channel_id=1, source_target_pairs={{0,8},{2,10},{4,12},{6,14},{8,0},{10,2},{12,4},{14,6},{16,24},{18,... | collective-permute-start | bytes 73736 | tf_op jit(solution)/shard_map/ppermute | solution.py:382
  53.9 5.6 %collective-permute-start.11 = (bf16[24,512]{1,0:T(8,128)(2,1)S(1)}, bf16[24,512]{1,0:T(8,128)(2,1)S(1)}, u32[]{:S(2)}, u32[]{:S(2)}) collective-permute-start(bf16[24,512]{1,0:T(8,128)(2,1)S(1)} %get-tuple-element.46), channel_id=1, source_target_pairs={{0,16},{2,18},{4,20},{6,22},{8,24},{10,26},{12,28},{14,30},{16,0},... | collective-permute-start | bytes 73736 | tf_op jit(solution)/shard_map/ppermute | solution.py:382
  57.7 5.6 %collective-permute-start.12 = (bf16[24,512]{1,0:T(8,128)(2,1)S(1)}, bf16[24,512]{1,0:T(8,128)(2,1)S(1)}, u32[]{:S(2)}, u32[]{:S(2)}) collective-permute-start(bf16[24,512]{1,0:T(8,128)(2,1)S(1)} %get-tuple-element.47), channel_id=1, source_target_pairs={{0,24},{2,26},{4,28},{6,30},{8,16},{10,18},{12,20},{14,22},{16,8},... | collective-permute-start | bytes 73736 | tf_op jit(solution)/shard_map/ppermute | solution.py:382

commit v2 on v1

v2 whole, which is shorter than its diff:
```python
import functools
import math

import jax
import jax.numpy as jnp
from jax import lax
from jax.experimental import pallas as pl
from jax.experimental.pallas import tpu as pltpu
from jax.sharding import PartitionSpec as P

F32, BF16 = jnp.float32, jnp.bfloat16
PLANE = 4
UNITS = 20
AHEAD = (2, 4, 1)
STREAM = 7
SECOND = 6
MORE = 3
SLOTS = 4
PIECES = 4
TILE = 512
MATRIX = 256
LANES = 128
TOP, TINY = 1440.0, 1e-30
SMALL = pl.CostEstimate(flops=1 << 20, bytes_accessed=1 << 20, transcendentals=0)
VMEM = 14 << 20


def select(rows, columns, source):
    row = lax.broadcasted_iota(jnp.int32, (rows, columns), 0)
    column = lax.broadcasted_iota(jnp.int32, (rows, columns), 1)
    return (column == source(row)).astype(BF16)


def copies(integral, start, unit, target, sems):
    step = target.shape[0] // PIECES
    return [
        pltpu.make_async_copy(
            integral.at[pl.ds(i * step, step), pl.ds(start, unit)],
            target.at[pl.ds(i * step, step), :],
            sems.at[i],
        )
        for i in range(PIECES)
    ]


def load(start, columns, unit, integral, after):
    depth = integral.shape[0]

    def kernel(integral_ref, after_ref, out_ref, sems):
        moves = []
        for k in range(columns // unit):
            target = out_ref.at[:, pl.ds(k * unit, unit)]
            moves += copies(integral_ref, start + k * unit, unit, target, sems.at[k])
        for move in moves:
            move.start()
        for move in moves:
            move.wait()

    return pl.pallas_call(
        kernel,
        out_shape=pltpu.VMEM((depth, columns), BF16),
        in_specs=[pl.BlockSpec(memory_space=pl.ANY)] * 2,
        out_specs=pl.BlockSpec(memory_space=pltpu.VMEM),
        scratch_shapes=[pltpu.SemaphoreType.DMA((columns // unit, PIECES))],
        compiler_params=pltpu.CompilerParams(vmem_limit_bytes=VMEM),
        cost_estimate=pl.CostEstimate(flops=0, bytes_accessed=depth * columns * 2, transcendentals=0),
    )(integral, after)


def encode(sums, largest):
    scale = (TOP / jnp.maximum(largest, TINY)).astype(BF16)
    scaled = sums * scale.astype(F32)
    square = scaled * scaled
    fourth = square * square
    return (fourth * fourth * square * (scaled * jnp.abs(scaled))).astype(BF16), scale


def decode(code, scale):
    code = code.astype(F32)
    size = jnp.exp2(jnp.log2(jnp.abs(code)) * (1.0 / 12.0)) * (1.0 / scale.astype(F32))
    return jnp.where(code < 0, -size, size)


def fold(group):
    return 8 // math.gcd(group, 8)


def window_row(row, group):
    whole = group // 8 * 8
    rest = group - whole
    if not rest:
        return row // group, row % group
    if not whole:
        return row // rest, row % rest
    behind = row - PLANE * whole
    tiled = behind < 0
    return jnp.where(tiled, row // whole, behind // rest), jnp.where(tiled, row % whole, whole + behind % rest)


def packed_rows(group, chip, part):
    whole = group // 8 * 8
    rest = group - whole
    rows = [(chip * whole, whole, part * whole)] if whole else []
    return rows + ([(PLANE * whole + chip * rest, rest, fold(group) * whole + part * rest)] if rest else [])


def unpacked(array, group, start, count):
    parts = fold(group)
    whole = group // 8 * 8
    rest = group - whole
    out = []
    for j in range(parts):
        pieces = []
        if start < whole:
            pieces.append(array[j * whole + start : j * whole + min(start + count, whole)])
        if start + count > whole:
            at = parts * whole + j * rest - whole
            pieces.append(array[at + max(start, whole) : at + start + count])
        out.append(pieces[0] if len(pieces) == 1 else jnp.concatenate(pieces, axis=0))
    return out


def split_by_plane(amplitudes, lines):
    pairs, blocks, offsets = amplitudes.shape
    group = lines * pairs

    def kernel(in_ref, *outs):
        me = lax.axis_index("ab")
        flat = in_ref[...].reshape(pairs * blocks, offsets)
        for r, out in enumerate(outs):

            def source(row):
                s, p = row // pairs, row % pairs
                return p * blocks + jnp.bitwise_xor(s * PLANE + r, me)

            taken = select(group, pairs * blocks, source)
            out[...] = jnp.dot(taken, flat, preferred_element_type=F32).astype(BF16)

    shape = jax.ShapeDtypeStruct((group, offsets), BF16)
    return pl.pallas_call(
        kernel,
        out_shape=[shape] * PLANE,
        in_specs=[pl.BlockSpec(memory_space=pltpu.VMEM)],
        out_specs=[pl.BlockSpec(memory_space=pltpu.VMEM)] * PLANE,
        compiler_params=pltpu.CompilerParams(vmem_limit_bytes=VMEM),
        cost_estimate=SMALL,
    )(amplitudes)


def split_by_line(parts, lines, pairs, after):
    group, offsets = parts[0].shape
    rows = PLANE * pairs

    def kernel(*refs):
        ins, outs = refs[:PLANE], refs[PLANE + 1 :]
        for s, out in enumerate(outs):
            total = 0.0
            for i, ref in enumerate(ins):
                r = (PLANE - i) % PLANE

                def source(row):
                    return jnp.where(row // pairs == r, s * pairs + row % pairs, -1)

                total += jnp.dot(select(rows, group, source), ref[...], preferred_element_type=F32)
            out[...] = total.astype(BF16)

    shape = jax.ShapeDtypeStruct((rows, offsets), BF16)
    return pl.pallas_call(
        kernel,
        out_shape=[shape] * lines,
        in_specs=[pl.BlockSpec(memory_space=pltpu.VMEM)] * PLANE + [pl.BlockSpec(memory_space=pl.ANY)],
        out_specs=[pl.BlockSpec(memory_space=pltpu.VMEM)] * lines,
        compiler_params=pltpu.CompilerParams(vmem_limit_bytes=VMEM),
        cost_estimate=SMALL,
    )(*parts, after)


def gather_half(parts, pairs, after):
    lines = len(parts)
    rows, offsets = parts[0].shape
    group = lines * pairs

    def kernel(*refs):
        total = 0.0
        for i in range(lines):
            s = (lines - i) % lines

            def source(row):
                r, at = window_row(row, group)
                return jnp.where(at // pairs == s, r * pairs + at % pairs, -1)

            total += jnp.dot(select(PLANE * group, rows, source), refs[i][...], preferred_element_type=F32)
        refs[-1][...] = total.astype(BF16)

    return pl.pallas_call(
        kernel,
        out_shape=jax.ShapeDtypeStruct((PLANE * group, offsets), BF16),
        in_specs=[pl.BlockSpec(memory_space=pltpu.VMEM)] * lines + [pl.BlockSpec(memory_space=pl.ANY)],
        out_specs=pl.BlockSpec(memory_space=pltpu.VMEM),
        compiler_params=pltpu.CompilerParams(vmem_limit_bytes=VMEM),
        cost_estimate=SMALL,
    )(*parts, after)


def join(halves, after):
    cores = len(halves)
    rows, offsets = halves[0].shape

    def kernel(*refs):
        core = lax.axis_index("cd")
        for c in range(cores):

            @pl.when(core == c)
            def _():
                for j in range(cores):
                    refs[-1][:, pl.ds((c ^ j) * offsets, offsets)] = refs[j][...]

    return pl.pallas_call(
        kernel,
        out_shape=jax.ShapeDtypeStruct((rows, cores * offsets), BF16),
        in_specs=[pl.BlockSpec(memory_space=pltpu.VMEM)] * cores + [pl.BlockSpec(memory_space=pl.ANY)],
        out_specs=pl.BlockSpec(memory_space=pltpu.VMEM),
        compiler_params=pltpu.CompilerParams(vmem_limit_bytes=VMEM),
        cost_estimate=SMALL,
    )(*halves, after)


def multiply(window_ref, chunk_ref, at, tile, sums):
    depth = window_ref.shape[1]
    if not sums:
        return [(0, jnp.dot(window_ref[...], chunk_ref[:, pl.ds(at, tile)], preferred_element_type=F32))]
    for k in range(depth // MATRIX):
        ks = pl.ds(k * MATRIX, MATRIX)
        for unit in range(2):
            pltpu.matmul_push_rhs(chunk_ref[ks, pl.ds(at + unit * MATRIX, MATRIX)], k % 2, unit)
        for unit in range(2):
            pltpu.matmul_acc_lhs(sums[unit], window_ref[:, ks], k % 2)
    return [(unit * MATRIX, pltpu.matmul_pop(sums[unit])) for unit in range(2)]


def product(window, integral, ready, start, stream, more, unit, after):
    group = window.shape[0] // PLANE
    depth = integral.shape[0]
    parts = fold(group)
    columns = sum(chunk.shape[1] for chunk in ready) + stream
    width = columns // parts
    tile = next(t for t in (TILE, 256, 128) if unit % t == 0)
    steps = stream // unit

    def kernel(window_ref, integral_ref, *refs):
        chunks, refs = refs[: len(ready)], refs[len(ready) + len(after) :]
        own, outs, refs = refs[0], refs[1:PLANE], refs[PLANE:]
        kept, ring, sems, more_sems = refs[-4:]
        incoming = [
            copies(integral_ref, start + k * unit, unit, ring.at[k % SLOTS], sems.at[k % SLOTS]) for k in range(steps)
        ]
        handed = [
            copies(integral_ref, start + stream + k * unit, unit, refs[0].at[:, pl.ds(k * unit, unit)], more_sems.at[k])
            for k in range(more // unit)
        ]
        for move in sum(incoming[: SLOTS - 1], []):
            move.start()

        def tiles(chunk_ref, column, sums):
            part, offset = divmod(column, width)
            for at in range(0, unit, tile):
                for place, values in multiply(window_ref, chunk_ref, at, tile, sums):
                    columns_at = pl.ds(offset + at + place, values.shape[1])
                    for r in range(PLANE):
                        target = own if r == 0 else kept.at[r - 1]
                        for begin, rows, where in packed_rows(group, r, part):
                            target[where : where + rows, columns_at] = values[begin : begin + rows]

        def work(*sums):
            sets = [sums[:2], sums[2:]]
            lead = len(held) if steps < SLOTS else 2
            for k in range(lead):
                tiles(held[k], k * unit, sets[k % 2])
            for k in range(max(len(held) - lead, steps)):
                if k < steps:
                    for move in incoming[k]:
                        move.wait()
                    for move in incoming[k + SLOTS - 1] if k + SLOTS - 1 < steps else []:
                        move.start()
                    tiles(ring.at[k % SLOTS], (len(held) + k) * unit, sets[0])
                if k + lead < len(held):
                    tiles(held[k + lead], (k + lead) * unit, sets[1])
                if k % 2 == 1 and k // 2 < len(handed):
                    for move in handed[k // 2]:
                        move.start()

        held = [
            chunk_ref.at[:, pl.ds(at, unit)] for chunk_ref in chunks for at in range(0, chunk_ref.shape[1], unit)
        ]
        rows = PLANE * group
        if tile == 2 * MATRIX and depth % MATRIX == 0 and rows % 16 == 0:
            pl.run_scoped(work, *[pltpu.ACC(i % 2)((rows, MATRIX), F32) for i in range(4)])
        else:
            work()

        largest = jnp.max(jnp.abs(kept[...]), axis=(0, 1, 2), keepdims=True)[0]
        for r, out in enumerate(outs):
            code, scale = encode(kept[r], largest)
            out[:, pl.ds(0, width)] = code
            out[:, pl.ds(width, LANES)] = jnp.broadcast_to(scale, (parts * group, LANES))
        for move in sum(handed, []):
            move.wait()

    shapes = [pltpu.VMEM((parts * group, width), F32)]
    shapes += [pltpu.VMEM((parts * group, width + LANES), BF16)] * (PLANE - 1)
    if more:
        shapes.append(pltpu.VMEM((depth, more), BF16))
    ready = [pltpu.with_memory_space_constraint(chunk, pltpu.VMEM) for chunk in ready]
    return pl.pallas_call(
        kernel,
        out_shape=shapes,
        in_specs=[pl.BlockSpec(memory_space=pltpu.VMEM), pl.BlockSpec(memory_space=pl.ANY)]
        + [pl.BlockSpec(memory_space=pltpu.VMEM)] * len(ready)
        + [pl.BlockSpec(memory_space=pl.ANY)] * len(after),
        out_specs=[pl.BlockSpec(memory_space=pltpu.VMEM)] * len(shapes),
        scratch_shapes=[
            pltpu.VMEM((PLANE - 1, parts * group, width), F32),
            pltpu.VMEM((min(SLOTS, steps), depth, unit), BF16),
            pltpu.SemaphoreType.DMA((min(SLOTS, steps), PIECES)),
            pltpu.SemaphoreType.DMA((max(more // unit, 1), PIECES)),
        ],
        compiler_params=pltpu.CompilerParams(vmem_limit_bytes=VMEM),
        cost_estimate=pl.CostEstimate(
            flops=2 * window.shape[0] * depth * columns, bytes_accessed=depth * columns * 2, transcendentals=0
        ),
    )(window, integral, *ready, *after)


def add_codes(chunk):
    rows, width = chunk[0].shape

    def kernel(own_ref, *refs):
        total = own_ref[...]
        for ref in refs[:-1]:
            total += decode(ref[:, pl.ds(0, width)], ref[:, pl.ds(width, 1)])
        refs[-1][...] = total

    return pl.pallas_call(
        kernel,
        out_shape=jax.ShapeDtypeStruct((rows, width), F32),
        in_specs=[pl.BlockSpec(memory_space=pltpu.VMEM)] * len(chunk),
        out_specs=pl.BlockSpec(memory_space=pltpu.VMEM),
        compiler_params=pltpu.CompilerParams(vmem_limit_bytes=VMEM),
        cost_estimate=SMALL,
    )(*chunk)


def line_fold(widths, parts):
    return next(n for n in (8, 4, 2, 1) if n * parts <= 8 and all(width % (n * LANES) == 0 for width in widths))


def add_plane(chunks, lines, pairs):
    group = lines * pairs
    parts = fold(group)
    widths = [own.shape[1] for own, *_ in chunks]
    pieces = line_fold(widths, parts)
    rows, columns = parts * pieces * pairs, sum(widths) // pieces

    def kernel(*refs):
        ins, own, outs, kept = list(refs[: -lines - 1]), refs[-lines - 1], refs[-lines:-1], refs[-1]
        start, largest = 0, jnp.zeros((1, 1), F32)
        for i, width in enumerate(widths):
            total = ins.pop(0)[...]
            for _ in chunks[i][1:]:
                ref = ins.pop(0)
                total += decode(ref[:, pl.ds(0, width)], ref[:, pl.ds(width, 1)])
            largest = jnp.maximum(largest, jnp.max(jnp.abs(total), keepdims=True))
            piece = width // pieces
            for s in range(lines):
                for j, part in enumerate(unpacked(total, group, s * pairs, pairs)):
                    for k in range(pieces):
                        row = pl.ds((j * pieces + k) * pairs, pairs)
                        value = part[:, k * piece : (k + 1) * piece]
                        if s == 0:
                            own[row, pl.ds(start, piece)] = value
                        else:
                            kept[s - 1, row, pl.ds(start, piece)] = value
            start += piece
        for s, out in enumerate(outs):
            code, scale = encode(kept[s], largest)
            out[:, pl.ds(0, columns)] = code
            out[:, pl.ds(columns, LANES)] = jnp.broadcast_to(scale, (rows, LANES))

    code = jax.ShapeDtypeStruct((rows, columns + LANES), BF16)
    return pl.pallas_call(
        kernel,
        out_shape=[jax.ShapeDtypeStruct((rows, columns), F32)] + [code] * (lines - 1),
        in_specs=[pl.BlockSpec(memory_space=pltpu.VMEM)] * sum(map(len, chunks)),
        out_specs=[pl.BlockSpec(memory_space=pltpu.VMEM)] * lines,
        scratch_shapes=[pltpu.VMEM((lines - 1, rows, columns), F32)],
        compiler_params=pltpu.CompilerParams(vmem_limit_bytes=VMEM),
        cost_estimate=SMALL,
    )(*[ref for chunk in chunks for ref in chunk])


def add_line(own, codes, widths, parts, pairs):
    rows, columns = own.shape
    pieces = line_fold(widths, parts)

    def kernel(own_ref, *refs):
        total = own_ref[...]
        for ref in refs[:-1]:
            total += decode(ref[:, pl.ds(0, columns)], ref[:, pl.ds(columns, 1)])
        at, start = 0, 0
        for width in widths:
            piece = width // pieces
            for j in range(parts * pieces):
                refs[-1][:, pl.ds(start, piece)] = total[j * pairs : (j + 1) * pairs, at : at + piece]
                start += piece
            at += piece

    return pl.pallas_call(
        kernel,
        out_shape=jax.ShapeDtypeStruct((pairs, sum(widths) * parts), F32),
        in_specs=[pl.BlockSpec(memory_space=pltpu.VMEM)] * (1 + len(codes)),
        out_specs=pl.BlockSpec(memory_space=pltpu.VMEM),
        compiler_params=pltpu.CompilerParams(vmem_limit_bytes=VMEM),
        cost_estimate=SMALL,
    )(own, *codes)


def per_device(owners, cores, amplitudes, integral):
    pairs = amplitudes.shape[0]
    lines = owners // PLANE
    def swap(axis, size, array, by):
        return lax.ppermute(array, axis, [(i, i ^ by) for i in range(size)])

    def farthest_first(exchange, arrays):
        return [exchange(array, i + 1) for i, array in enumerate(arrays)][::-1]

    plane = functools.partial(swap, "ab", owners)
    line = lambda array, by: swap("ab", owners, array, by * PLANE)
    core = functools.partial(swap, "cd", cores)

    unit = integral.shape[1] // UNITS
    early, middle, late = (count * unit for count in AHEAD)

    parts = split_by_plane(amplitudes, lines)
    ready = [load(0, early, unit, integral, parts[0])]
    parts = [parts[0]] + farthest_first(plane, parts[1:])
    parts = split_by_line(parts, lines, pairs, ready[-1])
    ready.append(load(early, middle, unit, integral, parts[0]))
    parts = [parts[0]] + farthest_first(line, parts[1:])
    half = gather_half(parts, pairs, ready[-1])
    ready.append(load(early + middle, late, unit, integral, half))
    window = join([half] + [core(half, j) for j in range(1, cores)], ready[-1])

    start, more = early + middle + late, MORE * unit
    own, *codes, chunk = product(window, integral, ready, start, STREAM * unit, more, unit, [])
    chunks = [[own] + farthest_first(plane, codes)]
    start += STREAM * unit + more
    own, *codes = product(window, integral, [chunk], start, SECOND * unit - more, 0, unit, [own])
    chunks.append([own] + farthest_first(plane, codes))
    chunks[0] = [add_codes(chunks[0])]
    own, *codes = add_plane(chunks, lines, pairs)
    codes = farthest_first(line, codes)
    return add_line(own, codes, [chunk[0].shape[1] for chunk in chunks], fold(lines * pairs), pairs)


def solution(mesh):
    placed = (P("ab", None, "cd"), P("ab", "cd"))
    return jax.shard_map(
        functools.partial(per_device, mesh.shape["ab"], mesh.shape["cd"]),
        mesh=mesh,
        in_specs=placed,
        out_specs=P("ab", "cd"),
        check_vma=False,
    )
```

time: 64.3 us -> 59.4 us (0.924)
  starting transfers between devices: 25.4 us -> 20.7 us
    ppermute x19 -> x16, starting transfers between devices: 25.4 us -> 20.7 us  [swap(): return lax.ppermute(array, axis, [(i, i ^ by) for i in range(size)])]
    pallas_call x2 -> x3, Pallas kernels: 8.67 us -> 9.66 us  [load(): pl.pallas_call(kernel, out_shape=pltpu.VMEM((depth, columns), BF16), in_s...]
    ppermute x19 -> x16, waiting for transfers between devices: 8.83 us -> 8.53 us  [swap(): return lax.ppermute(array, axis, [(i, i ^ by) for i in range(size)])]
    pallas_call x3 -> x4, Pallas kernels: 1.42 us -> 1.67 us  [the longest x1 0.85 us: add_line(): pl.pallas_call(kernel, out_shape=jax.ShapeDtypeStruct((pairs, sum(widths)...]
  transfers between devices with their start and end apart: 19 -> 16, of which waited for: 6 -> 8; matrix products, arithmetic and copies ran while one was open for 0% -> 0% of each run, Pallas kernels for 25% -> 27%
where the time goes in v2:
time: 59.4 us; the launch traced here: 59.3 us
  Pallas kernels  29 us (49%)
  starting transfers between devices  20.7 us (35%)
  waiting for transfers between devices  8.53 us (14%)
  local copies, waits for them, and re-layouts  0.91 us (2%)
    ppermute x16, starting transfers between devices, swap(): return lax.ppermute(array, axis, [(i, i ^ by) for i in range(size)])  20.7 us
    pallas_call x2, Pallas kernels, product(): pl.pallas_call(kernel, out_shape=shapes, in_specs=[pl.BlockSpec(memory_sp...  16.6 us
    pallas_call x3, Pallas kernels, load(): pl.pallas_call(kernel, out_shape=pltpu.VMEM((depth, columns), BF16), in_s...  9.66 us
    ppermute x16, waiting for transfers between devices, swap(): return lax.ppermute(array, axis, [(i, i ^ by) for i in range(size)])  8.53 us
  transfers between devices with their start and end apart: 16, of which 8 were waited for; matrix products, arithmetic and copies ran while one was open for 0% of the time, Pallas kernels for 27%

profile of v2, /device:TPU:0, one launch (start us, length us, event | category | flops | bytes accessed | tf_op | source)
XLA Modules:
  0.0 59.3 jit_solution(2079341940566714819)
XLA Ops:
  0.0 0.9 %copy-done = bf16[3,16,1536]{2,1,0:T(8,128)(2,1)S(1)} copy-done((bf16[3,16,1536]{2,1,0:T(8,128)(2,1)S(1)}, bf16[3,16,1536]{2,1,0:T(8,128)(2,1)}, u32[]{:S(2)}) %copy-start) | copy-done | bytes 147480
  0.9 0.2 shard_map.28
  1.1 4.0 %collective-permute-start = (bf16[12,1536]{1,0:T(8,128)(2,1)S(1)}, bf16[12,1536]{1,0:T(8,128)(2,1)S(1)}, u32[]{:S(2)}, u32[]{:S(2)}) collective-permute-start(bf16[12,1536]{1,0:T(8,128)(2,1)S(1)} %get-tuple-element.27), channel_id=1, source_target_pairs={{0,6},{2,4},{4,2},{6,0},{8,14},{10,12},{12,10},{14,8},{16,22},{18,... | collective-permute-start | bytes 110600 | tf_op jit(solution)/shard_map/ppermute | solution.py:431
  5.1 0.5 collective-permute-start.1
  5.7 2.9 %shard_map.29.refs_4_.refs_0_ = bf16[3072,1024]{1,0:T(8,128)(2,1)S(1)} custom-call(bf16[3072,10240]{1,0:T(8,128)(2,1)} %integral_ref.9, bf16[12,1536]{1,0:T(8,128)(2,1)S(1)} %get-tuple-element.26.after_ref.refs_0_), custom_call_target="tpu_custom_call" | custom-call | bytes 6291456 | tf_op jit(solution)/shard_map/pallas_call | solution.py:59
  8.6 0.5 collective-permute-done.1.refs_2_
  9.2 0.5 collective-permute-done.2.refs_3_
  9.7 0.3 shard_map.30
  10.0 3.7 %collective-permute-start.3 = (bf16[12,1536]{1,0:T(8,128)(2,1)S(1)}, bf16[12,1536]{1,0:T(8,128)(2,1)S(1)}, u32[]{:S(2)}, u32[]{:S(2)}) collective-permute-start(bf16[12,1536]{1,0:T(8,128)(2,1)S(1)} %get-tuple-element.31), channel_id=1, source_target_pairs={{0,24},{2,26},{4,28},{6,30},{8,16},{10,18},{12,20},{14,22},{16,8},... | collective-permute-start | bytes 110600 | tf_op jit(solution)/shard_map/ppermute | solution.py:431
  13.7 0.8 %collective-permute-start.5 = (bf16[12,1536]{1,0:T(8,128)(2,1)S(1)}, bf16[12,1536]{1,0:T(8,128)(2,1)S(1)}, u32[]{:S(2)}, u32[]{:S(2)}) collective-permute-start(bf16[12,1536]{1,0:T(8,128)(2,1)S(1)} %get-tuple-element.33), channel_id=1, source_target_pairs={{0,8},{2,10},{4,12},{6,14},{8,0},{10,2},{12,4},{14,6},{16,24},{18,... | collective-permute-start | bytes 110600 | tf_op jit(solution)/shard_map/ppermute | solution.py:431
  14.5 4.8 %shard_map.31.refs_4_.refs_1_ = bf16[3072,2048]{1,0:T(8,128)(2,1)S(1)} custom-call(bf16[3072,10240]{1,0:T(8,128)(2,1)} %integral_ref.9, bf16[12,1536]{1,0:T(8,128)(2,1)S(1)} %get-tuple-element.30.after_ref.refs_0_), custom_call_target="tpu_custom_call" | custom-call | bytes 12582912 | tf_op jit(solution)/shard_map/pallas_call | solution.py:59
  19.3 0.3 shard_map.32.after_ref.refs_0_
  19.7 1.9 %shard_map.33.refs_2_ = bf16[3072,512]{1,0:T(8,128)(2,1)S(1)} custom-call(bf16[3072,10240]{1,0:T(8,128)(2,1)} %integral_ref.9, bf16[48,1536]{1,0:T(8,128)(2,1)S(1)} %shard_map.32.after_ref.refs_0_), custom_call_target="tpu_custom_call" | custom-call | bytes 3145728 | tf_op jit(solution)/shard_map/pallas_call | solution.py:59
  21.7 10.7 %shard_map.35 = (f32[24,3584]{1,0:T(8,128)S(1)}, bf16[24,3712]{1,0:T(8,128)(2,1)S(1)}, bf16[24,3712]{1,0:T(8,128)(2,1)S(1)}, bf16[24,3712]{1,0:T(8,128)(2,1)S(1)}, bf16[3072,1536]{1,0:T(8,128)(2,1)S(1)}) custom-call(bf16[48,3072]{1,0:T(8,128)(2,1)S(1)} %shard_map.34.window_ref, bf16[3072,10240]{1,0:T(8,128)(2,1)} %integral_ref.9, ...), custom_call_target="tpu_custom_call" | custom-call | flops 2113929216 | bytes 44040192 | tf_op jit(solution)/shard_map/pallas_call | solution.py:314
  32.4 1.9 %collective-permute-start.7 = (bf16[24,3712]{1,0:T(8,128)(2,1)S(1)}, bf16[24,3712]{1,0:T(8,128)(2,1)S(1)}, u32[]{:S(2)}, u32[]{:S(2)}) collective-permute-start(bf16[24,3712]{1,0:T(8,128)(2,1)S(1)} %get-tuple-element.35), channel_id=1, source_target_pairs={{0,6},{2,4},{4,2},{6,0},{8,14},{10,12},{12,10},{14,8},{16,22},{18,... | collective-permute-start | bytes 534536 | tf_op jit(solution)/shard_map/ppermute | solution.py:431
  34.3 0.5 collective-permute-start.8
  34.8 1.2 %collective-permute-start.9 = (bf16[24,3712]{1,0:T(8,128)(2,1)S(1)}, bf16[24,3712]{1,0:T(8,128)(2,1)S(1)}, u32[]{:S(2)}, u32[]{:S(2)}) collective-permute-start(bf16[24,3712]{1,0:T(8,128)(2,1)S(1)} %get-tuple-element.37), channel_id=1, source_target_pairs={{0,2},{2,0},{4,6},{6,4},{8,10},{10,8},{12,14},{14,12},{16,18},{18,... | collective-permute-start | bytes 534536 | tf_op jit(solution)/shard_map/ppermute | solution.py:431
  36.0 5.9 %shard_map.37 = (f32[24,1536]{1,0:T(8,128)S(1)}, bf16[24,1664]{1,0:T(8,128)(2,1)S(1)}, bf16[24,1664]{1,0:T(8,128)(2,1)S(1)}, bf16[24,1664]{1,0:T(8,128)(2,1)S(1)}) custom-call(bf16[48,3072]{1,0:T(8,128)(2,1)S(1)} %shard_map.34.window_ref, bf16[3072,10240]{1,0:T(8,128)(2,1)} %integral_ref.9, bf16[3072,1536]{1,0:T(8,128)(2,1)S(1)} %get-tuple-element.38.refs_0_, ...), custom_call_target="tpu_custom_call" | custom-call | flops 905969664 | bytes 18874368 | tf_op jit(solution)/shard_map/pallas_call | solution.py:314
  41.9 1.9 %collective-permute-start.10 = (bf16[24,1664]{1,0:T(8,128)(2,1)S(1)}, bf16[24,1664]{1,0:T(8,128)(2,1)S(1)}, u32[]{:S(2)}, u32[]{:S(2)}) collective-permute-start(bf16[24,1664]{1,0:T(8,128)(2,1)S(1)} %get-tuple-element.40), channel_id=1, source_target_pairs={{0,6},{2,4},{4,2},{6,0},{8,14},{10,12},{12,10},{14,8},{16,22},{18,... | collective-permute-start | bytes 239624 | tf_op jit(solution)/shard_map/ppermute | solution.py:431
  43.8 0.5 collective-permute-start.11
  44.3 1.2 %collective-permute-start.12 = (bf16[24,1664]{1,0:T(8,128)(2,1)S(1)}, bf16[24,1664]{1,0:T(8,128)(2,1)S(1)}, u32[]{:S(2)}, u32[]{:S(2)}) collective-permute-start(bf16[24,1664]{1,0:T(8,128)(2,1)S(1)} %get-tuple-element.42), channel_id=1, source_target_pairs={{0,2},{2,0},{4,6},{6,4},{8,10},{10,8},{12,14},{14,12},{16,18},{18,... | collective-permute-start | bytes 239624 | tf_op jit(solution)/shard_map/ppermute | solution.py:431
  45.5 0.5 shard_map.36.refs_0_
  46.0 1.7 %collective-permute-done.10.refs_2_ = bf16[24,1664]{1,0:T(8,128)(2,1)S(1)} collective-permute-done((bf16[24,1664]{1,0:T(8,128)(2,1)S(1)}, bf16[24,1664]{1,0:T(8,128)(2,1)S(1)}, u32[]{:S(2)}, u32[]{:S(2)}) %collective-permute-start.10) | collective-permute-done | bytes 79904 | tf_op jit(solution)/shard_map/ppermute | solution.py:431
  47.7 0.8 %collective-permute-done.11.refs_3_ = bf16[24,1664]{1,0:T(8,128)(2,1)S(1)} collective-permute-done((bf16[24,1664]{1,0:T(8,128)(2,1)S(1)}, bf16[24,1664]{1,0:T(8,128)(2,1)S(1)}, u32[]{:S(2)}, u32[]{:S(2)}) %collective-permute-start.11) | collective-permute-done | bytes 79904 | tf_op jit(solution)/shard_map/ppermute | solution.py:431
  48.6 0.2 collective-permute-done.12.refs_4_
  48.8 0.5 shard_map.38
  49.3 3.7 %collective-permute-start.13 = (bf16[24,1408]{1,0:T(8,128)(2,1)S(1)}, bf16[24,1408]{1,0:T(8,128)(2,1)S(1)}, u32[]{:S(2)}, u32[]{:S(2)}) collective-permute-start(bf16[24,1408]{1,0:T(8,128)(2,1)S(1)} %get-tuple-element.44), channel_id=1, source_target_pairs={{0,24},{2,26},{4,28},{6,30},{8,16},{10,18},{12,20},{14,22},{16,8},... | collective-permute-start | bytes 202760 | tf_op jit(solution)/shard_map/ppermute | solution.py:431
  52.9 0.8 %collective-permute-start.15 = (bf16[24,1408]{1,0:T(8,128)(2,1)S(1)}, bf16[24,1408]{1,0:T(8,128)(2,1)S(1)}, u32[]{:S(2)}, u32[]{:S(2)}) collective-permute-start(bf16[24,1408]{1,0:T(8,128)(2,1)S(1)} %get-tuple-element.46), channel_id=1, source_target_pairs={{0,8},{2,10},{4,12},{6,14},{8,0},{10,2},{12,4},{14,6},{16,24},{18,... | collective-permute-start | bytes 202760 | tf_op jit(solution)/shard_map/ppermute | solution.py:431
  53.7 1.8 %collective-permute-done.13.refs_0_ = bf16[24,1408]{1,0:T(8,128)(2,1)S(1)} collective-permute-done((bf16[24,1408]{1,0:T(8,128)(2,1)S(1)}, bf16[24,1408]{1,0:T(8,128)(2,1)S(1)}, u32[]{:S(2)}, u32[]{:S(2)}) %collective-permute-start.13) | collective-permute-done | bytes 67616 | tf_op jit(solution)/shard_map/ppermute | solution.py:431
  55.5 2.6 %collective-permute-done.14.refs_1_ = bf16[24,1408]{1,0:T(8,128)(2,1)S(1)} collective-permute-done((bf16[24,1408]{1,0:T(8,128)(2,1)S(1)}, bf16[24,1408]{1,0:T(8,128)(2,1)S(1)}, u32[]{:S(2)}, u32[]{:S(2)}) %collective-permute-start.14) | collective-permute-done | bytes 67616 | tf_op jit(solution)/shard_map/ppermute | solution.py:431
  58.2 0.2 collective-permute-done.15.refs_2_
  58.4 0.8 %shard_map.39 = f32[3,10240]{1,0:T(4,128)} custom-call(f32[24,1280]{1,0:T(8,128)S(1)} %get-tuple-element.43.own_ref, bf16[24,1408]{1,0:T(8,128)(2,1)S(1)} %collective-permute-done.13.refs_0_, bf16[24,1408]{1,0:T(8,128)(2,1)S(1)} %collective-permute-done.14.refs_1_, bf16[24,1408]{1,0:T(8,128)(2,1)S(1)} %collective-permute-done.15.refs_2_), custom_call_target="tpu_custom_call" | custom-call | flops 1048576 | bytes 1048576 | tf_op jit(solution)/shard_map/pallas_call | solution.py:417
  (14 shorter events, 0.3 us)
Async XLA Ops:
  0.0 0.9 %copy-start = (bf16[3,16,1536]{2,1,0:T(8,128)(2,1)S(1)}, bf16[3,16,1536]{2,1,0:T(8,128)(2,1)}, u32[]{:S(2)}) copy-start(bf16[3,16,1536]{2,1,0:T(8,128)(2,1)} %in_ref.1) | copy-start | bytes 442372
  1.1 7.5 %collective-permute-start = (bf16[12,1536]{1,0:T(8,128)(2,1)S(1)}, bf16[12,1536]{1,0:T(8,128)(2,1)S(1)}, u32[]{:S(2)}, u32[]{:S(2)}) collective-permute-start(bf16[12,1536]{1,0:T(8,128)(2,1)S(1)} %get-tuple-element.27), channel_id=1, source_target_pairs={{0,6},{2,4},{4,2},{6,0},{8,14},{10,12},{12,10},{14,8},{16,22},{18,... | collective-permute-start | bytes 110600 | tf_op jit(solution)/shard_map/ppermute | solution.py:431
  5.1 4.1 %collective-permute-start.1 = (bf16[12,1536]{1,0:T(8,128)(2,1)S(1)}, bf16[12,1536]{1,0:T(8,128)(2,1)S(1)}, u32[]{:S(2)}, u32[]{:S(2)}) collective-permute-start(bf16[12,1536]{1,0:T(8,128)(2,1)S(1)} %get-tuple-element.28), channel_id=1, source_target_pairs={{0,4},{2,6},{4,0},{6,2},{8,12},{10,14},{12,8},{14,10},{16,20},{18,... | collective-permute-start | bytes 110600 | tf_op jit(solution)/shard_map/ppermute | solution.py:431
  5.6 4.1 %collective-permute-start.2 = (bf16[12,1536]{1,0:T(8,128)(2,1)S(1)}, bf16[12,1536]{1,0:T(8,128)(2,1)S(1)}, u32[]{:S(2)}, u32[]{:S(2)}) collective-permute-start(bf16[12,1536]{1,0:T(8,128)(2,1)S(1)} %get-tuple-element.29), channel_id=1, source_target_pairs={{0,2},{2,0},{4,6},{6,4},{8,10},{10,8},{12,14},{14,12},{16,18},{18,... | collective-permute-start | bytes 110600 | tf_op jit(solution)/shard_map/ppermute | solution.py:431
  10.0 9.3 %collective-permute-start.3 = (bf16[12,1536]{1,0:T(8,128)(2,1)S(1)}, bf16[12,1536]{1,0:T(8,128)(2,1)S(1)}, u32[]{:S(2)}, u32[]{:S(2)}) collective-permute-start(bf16[12,1536]{1,0:T(8,128)(2,1)S(1)} %get-tuple-element.31), channel_id=1, source_target_pairs={{0,24},{2,26},{4,28},{6,30},{8,16},{10,18},{12,20},{14,22},{16,8},... | collective-permute-start | bytes 110600 | tf_op jit(solution)/shard_map/ppermute | solution.py:431
  13.7 5.6 %collective-permute-start.4 = (bf16[12,1536]{1,0:T(8,128)(2,1)S(1)}, bf16[12,1536]{1,0:T(8,128)(2,1)S(1)}, u32[]{:S(2)}, u32[]{:S(2)}) collective-permute-start(bf16[12,1536]{1,0:T(8,128)(2,1)S(1)} %get-tuple-element.32), channel_id=1, source_target_pairs={{0,16},{2,18},{4,20},{6,22},{8,24},{10,26},{12,28},{14,30},{16,0},... | collective-permute-start | bytes 110600 | tf_op jit(solution)/shard_map/ppermute | solution.py:431
  13.7 5.6 %collective-permute-start.5 = (bf16[12,1536]{1,0:T(8,128)(2,1)S(1)}, bf16[12,1536]{1,0:T(8,128)(2,1)S(1)}, u32[]{:S(2)}, u32[]{:S(2)}) collective-permute-start(bf16[12,1536]{1,0:T(8,128)(2,1)S(1)} %get-tuple-element.33), channel_id=1, source_target_pairs={{0,8},{2,10},{4,12},{6,14},{8,0},{10,2},{12,4},{14,6},{16,24},{18,... | collective-permute-start | bytes 110600 | tf_op jit(solution)/shard_map/ppermute | solution.py:431
  19.6 2.0 %collective-permute-start.6 = (bf16[48,1536]{1,0:T(8,128)(2,1)S(1)}, bf16[48,1536]{1,0:T(8,128)(2,1)S(1)}, u32[]{:S(2)}, u32[]{:S(2)}) collective-permute-start(bf16[48,1536]{1,0:T(8,128)(2,1)S(1)} %shard_map.32.after_ref.refs_0_), channel_id=1, source_target_pairs={{0,1},{1,0},{2,3},{3,2},{4,5},{5,4},{6,7},{7,6},{8,9},{9,8},{10,11... | collective-permute-start | bytes 442376 | tf_op jit(solution)/shard_map/ppermute | solution.py:431
  32.4 11.9 %collective-permute-start.7 = (bf16[24,3712]{1,0:T(8,128)(2,1)S(1)}, bf16[24,3712]{1,0:T(8,128)(2,1)S(1)}, u32[]{:S(2)}, u32[]{:S(2)}) collective-permute-start(bf16[24,3712]{1,0:T(8,128)(2,1)S(1)} %get-tuple-element.35), channel_id=1, source_target_pairs={{0,6},{2,4},{4,2},{6,0},{8,14},{10,12},{12,10},{14,8},{16,22},{18,... | collective-permute-start | bytes 534536 | tf_op jit(solution)/shard_map/ppermute | solution.py:431
  34.3 11.2 %collective-permute-start.8 = (bf16[24,3712]{1,0:T(8,128)(2,1)S(1)}, bf16[24,3712]{1,0:T(8,128)(2,1)S(1)}, u32[]{:S(2)}, u32[]{:S(2)}) collective-permute-start(bf16[24,3712]{1,0:T(8,128)(2,1)S(1)} %get-tuple-element.36), channel_id=1, source_target_pairs={{0,4},{2,6},{4,0},{6,2},{8,12},{10,14},{12,8},{14,10},{16,20},{18,... | collective-permute-start | bytes 534536 | tf_op jit(solution)/shard_map/ppermute | solution.py:431
  34.8 10.7 %collective-permute-start.9 = (bf16[24,3712]{1,0:T(8,128)(2,1)S(1)}, bf16[24,3712]{1,0:T(8,128)(2,1)S(1)}, u32[]{:S(2)}, u32[]{:S(2)}) collective-permute-start(bf16[24,3712]{1,0:T(8,128)(2,1)S(1)} %get-tuple-element.37), channel_id=1, source_target_pairs={{0,2},{2,0},{4,6},{6,4},{8,10},{10,8},{12,14},{14,12},{16,18},{18,... | collective-permute-start | bytes 534536 | tf_op jit(solution)/shard_map/ppermute | solution.py:431
  41.9 5.8 %collective-permute-start.10 = (bf16[24,1664]{1,0:T(8,128)(2,1)S(1)}, bf16[24,1664]{1,0:T(8,128)(2,1)S(1)}, u32[]{:S(2)}, u32[]{:S(2)}) collective-permute-start(bf16[24,1664]{1,0:T(8,128)(2,1)S(1)} %get-tuple-element.40), channel_id=1, source_target_pairs={{0,6},{2,4},{4,2},{6,0},{8,14},{10,12},{12,10},{14,8},{16,22},{18,... | collective-permute-start | bytes 239624 | tf_op jit(solution)/shard_map/ppermute | solution.py:431
  43.8 4.7 %collective-permute-start.11 = (bf16[24,1664]{1,0:T(8,128)(2,1)S(1)}, bf16[24,1664]{1,0:T(8,128)(2,1)S(1)}, u32[]{:S(2)}, u32[]{:S(2)}) collective-permute-start(bf16[24,1664]{1,0:T(8,128)(2,1)S(1)} %get-tuple-element.41), channel_id=1, source_target_pairs={{0,4},{2,6},{4,0},{6,2},{8,12},{10,14},{12,8},{14,10},{16,20},{18,... | collective-permute-start | bytes 239624 | tf_op jit(solution)/shard_map/ppermute | solution.py:431
  44.3 4.4 %collective-permute-start.12 = (bf16[24,1664]{1,0:T(8,128)(2,1)S(1)}, bf16[24,1664]{1,0:T(8,128)(2,1)S(1)}, u32[]{:S(2)}, u32[]{:S(2)}) collective-permute-start(bf16[24,1664]{1,0:T(8,128)(2,1)S(1)} %get-tuple-element.42), channel_id=1, source_target_pairs={{0,2},{2,0},{4,6},{6,4},{8,10},{10,8},{12,14},{14,12},{16,18},{18,... | collective-permute-start | bytes 239624 | tf_op jit(solution)/shard_map/ppermute | solution.py:431
  49.3 6.3 %collective-permute-start.13 = (bf16[24,1408]{1,0:T(8,128)(2,1)S(1)}, bf16[24,1408]{1,0:T(8,128)(2,1)S(1)}, u32[]{:S(2)}, u32[]{:S(2)}) collective-permute-start(bf16[24,1408]{1,0:T(8,128)(2,1)S(1)} %get-tuple-element.44), channel_id=1, source_target_pairs={{0,24},{2,26},{4,28},{6,30},{8,16},{10,18},{12,20},{14,22},{16,8},... | collective-permute-start | bytes 202760 | tf_op jit(solution)/shard_map/ppermute | solution.py:431
  52.9 5.2 %collective-permute-start.14 = (bf16[24,1408]{1,0:T(8,128)(2,1)S(1)}, bf16[24,1408]{1,0:T(8,128)(2,1)S(1)}, u32[]{:S(2)}, u32[]{:S(2)}) collective-permute-start(bf16[24,1408]{1,0:T(8,128)(2,1)S(1)} %get-tuple-element.45), channel_id=1, source_target_pairs={{0,16},{2,18},{4,20},{6,22},{8,24},{10,26},{12,28},{14,30},{16,0},... | collective-permute-start | bytes 202760 | tf_op jit(solution)/shard_map/ppermute | solution.py:431
  52.9 5.5 %collective-permute-start.15 = (bf16[24,1408]{1,0:T(8,128)(2,1)S(1)}, bf16[24,1408]{1,0:T(8,128)(2,1)S(1)}, u32[]{:S(2)}, u32[]{:S(2)}) collective-permute-start(bf16[24,1408]{1,0:T(8,128)(2,1)S(1)} %get-tuple-element.46), channel_id=1, source_target_pairs={{0,8},{2,10},{4,12},{6,14},{8,0},{10,2},{12,4},{14,6},{16,24},{18,... | collective-permute-start | bytes 202760 | tf_op jit(solution)/shard_map/ppermute | solution.py:431

commit v3 on v2

--- a/solution.py
+++ b/solution.py
@@ -258,7 +258,8 @@
             copies(integral_ref, start + stream + k * unit, unit, refs[0].at[:, pl.ds(k * unit, unit)], more_sems.at[k])
             for k in range(more // unit)
         ]
-        for move in sum(incoming[: SLOTS - 1], []):
+        ahead = min(SLOTS - 1, steps)
+        for move in incoming[0]:
             move.start()
 
         def tiles(chunk_ref, column, sums):
@@ -276,6 +277,8 @@
             lead = len(held) if steps < SLOTS else 2
             for k in range(lead):
                 tiles(held[k], k * unit, sets[k % 2])
+                for move in incoming[k + 1] if k + 1 < ahead else []:
+                    move.start()
             for k in range(max(len(held) - lead, steps)):
                 if k < steps:
                     for move in incoming[k]:

time: 59.4 us -> 59.4 us (level)
  no operation moved by 1% of the time
where the time goes in v3:
time: 59.4 us; the launch traced here: 59.3 us
  Pallas kernels  29 us (49%)
  starting transfers between devices  20.7 us (35%)
  waiting for transfers between devices  8.53 us (14%)
  local copies, waits for them, and re-layouts  0.91 us (2%)
    ppermute x16, starting transfers between devices, swap(): return lax.ppermute(array, axis, [(i, i ^ by) for i in range(size)])  20.7 us
    pallas_call x2, Pallas kernels, product(): pl.pallas_call(kernel, out_shape=shapes, in_specs=[pl.BlockSpec(memory_sp...  16.6 us
    pallas_call x3, Pallas kernels, load(): pl.pallas_call(kernel, out_shape=pltpu.VMEM((depth, columns), BF16), in_s...  9.66 us
    ppermute x16, waiting for transfers between devices, swap(): return lax.ppermute(array, axis, [(i, i ^ by) for i in range(size)])  8.53 us
  transfers between devices with their start and end apart: 16, of which 8 were waited for; matrix products, arithmetic and copies ran while one was open for 0% of the time, Pallas kernels for 27%

profile of v3, /device:TPU:0, one launch (start us, length us, event | category | flops | bytes accessed | tf_op | source)
XLA Modules:
  0.0 59.3 jit_solution(2079341940566714819)
XLA Ops:
  0.0 0.9 %copy-done = bf16[3,16,1536]{2,1,0:T(8,128)(2,1)S(1)} copy-done((bf16[3,16,1536]{2,1,0:T(8,128)(2,1)S(1)}, bf16[3,16,1536]{2,1,0:T(8,128)(2,1)}, u32[]{:S(2)}) %copy-start) | copy-done | bytes 147480
  0.9 0.2 shard_map.28
  1.1 4.0 %collective-permute-start = (bf16[12,1536]{1,0:T(8,128)(2,1)S(1)}, bf16[12,1536]{1,0:T(8,128)(2,1)S(1)}, u32[]{:S(2)}, u32[]{:S(2)}) collective-permute-start(bf16[12,1536]{1,0:T(8,128)(2,1)S(1)} %get-tuple-element.27), channel_id=1, source_target_pairs={{0,6},{2,4},{4,2},{6,0},{8,14},{10,12},{12,10},{14,8},{16,22},{18,... | collective-permute-start | bytes 110600 | tf_op jit(solution)/shard_map/ppermute | solution.py:434
  5.1 0.5 collective-permute-start.1
  5.7 2.9 %shard_map.29.refs_4_.refs_0_ = bf16[3072,1024]{1,0:T(8,128)(2,1)S(1)} custom-call(bf16[3072,10240]{1,0:T(8,128)(2,1)} %integral_ref.9, bf16[12,1536]{1,0:T(8,128)(2,1)S(1)} %get-tuple-element.26.after_ref.refs_0_), custom_call_target="tpu_custom_call" | custom-call | bytes 6291456 | tf_op jit(solution)/shard_map/pallas_call | solution.py:59
  8.6 0.5 collective-permute-done.1.refs_2_
  9.2 0.5 collective-permute-done.2.refs_3_
  9.7 0.3 shard_map.30
  10.0 3.7 %collective-permute-start.3 = (bf16[12,1536]{1,0:T(8,128)(2,1)S(1)}, bf16[12,1536]{1,0:T(8,128)(2,1)S(1)}, u32[]{:S(2)}, u32[]{:S(2)}) collective-permute-start(bf16[12,1536]{1,0:T(8,128)(2,1)S(1)} %get-tuple-element.31), channel_id=1, source_target_pairs={{0,24},{2,26},{4,28},{6,30},{8,16},{10,18},{12,20},{14,22},{16,8},... | collective-permute-start | bytes 110600 | tf_op jit(solution)/shard_map/ppermute | solution.py:434
  13.7 0.8 %collective-permute-start.5 = (bf16[12,1536]{1,0:T(8,128)(2,1)S(1)}, bf16[12,1536]{1,0:T(8,128)(2,1)S(1)}, u32[]{:S(2)}, u32[]{:S(2)}) collective-permute-start(bf16[12,1536]{1,0:T(8,128)(2,1)S(1)} %get-tuple-element.33), channel_id=1, source_target_pairs={{0,8},{2,10},{4,12},{6,14},{8,0},{10,2},{12,4},{14,6},{16,24},{18,... | collective-permute-start | bytes 110600 | tf_op jit(solution)/shard_map/ppermute | solution.py:434
  14.5 4.8 %shard_map.31.refs_4_.refs_1_ = bf16[3072,2048]{1,0:T(8,128)(2,1)S(1)} custom-call(bf16[3072,10240]{1,0:T(8,128)(2,1)} %integral_ref.9, bf16[12,1536]{1,0:T(8,128)(2,1)S(1)} %get-tuple-element.30.after_ref.refs_0_), custom_call_target="tpu_custom_call" | custom-call | bytes 12582912 | tf_op jit(solution)/shard_map/pallas_call | solution.py:59
  19.3 0.3 shard_map.32.after_ref.refs_0_
  19.7 1.9 %shard_map.33.refs_2_ = bf16[3072,512]{1,0:T(8,128)(2,1)S(1)} custom-call(bf16[3072,10240]{1,0:T(8,128)(2,1)} %integral_ref.9, bf16[48,1536]{1,0:T(8,128)(2,1)S(1)} %shard_map.32.after_ref.refs_0_), custom_call_target="tpu_custom_call" | custom-call | bytes 3145728 | tf_op jit(solution)/shard_map/pallas_call | solution.py:59
  21.7 10.7 %shard_map.35 = (f32[24,3584]{1,0:T(8,128)S(1)}, bf16[24,3712]{1,0:T(8,128)(2,1)S(1)}, bf16[24,3712]{1,0:T(8,128)(2,1)S(1)}, bf16[24,3712]{1,0:T(8,128)(2,1)S(1)}, bf16[3072,1536]{1,0:T(8,128)(2,1)S(1)}) custom-call(bf16[48,3072]{1,0:T(8,128)(2,1)S(1)} %shard_map.34.window_ref, bf16[3072,10240]{1,0:T(8,128)(2,1)} %integral_ref.9, ...), custom_call_target="tpu_custom_call" | custom-call | flops 2113929216 | bytes 44040192 | tf_op jit(solution)/shard_map/pallas_call | solution.py:317
  32.4 1.9 %collective-permute-start.7 = (bf16[24,3712]{1,0:T(8,128)(2,1)S(1)}, bf16[24,3712]{1,0:T(8,128)(2,1)S(1)}, u32[]{:S(2)}, u32[]{:S(2)}) collective-permute-start(bf16[24,3712]{1,0:T(8,128)(2,1)S(1)} %get-tuple-element.35), channel_id=1, source_target_pairs={{0,6},{2,4},{4,2},{6,0},{8,14},{10,12},{12,10},{14,8},{16,22},{18,... | collective-permute-start | bytes 534536 | tf_op jit(solution)/shard_map/ppermute | solution.py:434
  34.3 0.5 collective-permute-start.8
  34.8 1.2 %collective-permute-start.9 = (bf16[24,3712]{1,0:T(8,128)(2,1)S(1)}, bf16[24,3712]{1,0:T(8,128)(2,1)S(1)}, u32[]{:S(2)}, u32[]{:S(2)}) collective-permute-start(bf16[24,3712]{1,0:T(8,128)(2,1)S(1)} %get-tuple-element.37), channel_id=1, source_target_pairs={{0,2},{2,0},{4,6},{6,4},{8,10},{10,8},{12,14},{14,12},{16,18},{18,... | collective-permute-start | bytes 534536 | tf_op jit(solution)/shard_map/ppermute | solution.py:434
  36.0 5.9 %shard_map.37 = (f32[24,1536]{1,0:T(8,128)S(1)}, bf16[24,1664]{1,0:T(8,128)(2,1)S(1)}, bf16[24,1664]{1,0:T(8,128)(2,1)S(1)}, bf16[24,1664]{1,0:T(8,128)(2,1)S(1)}) custom-call(bf16[48,3072]{1,0:T(8,128)(2,1)S(1)} %shard_map.34.window_ref, bf16[3072,10240]{1,0:T(8,128)(2,1)} %integral_ref.9, bf16[3072,1536]{1,0:T(8,128)(2,1)S(1)} %get-tuple-element.38.refs_0_, ...), custom_call_target="tpu_custom_call" | custom-call | flops 905969664 | bytes 18874368 | tf_op jit(solution)/shard_map/pallas_call | solution.py:317
  41.9 1.9 %collective-permute-start.10 = (bf16[24,1664]{1,0:T(8,128)(2,1)S(1)}, bf16[24,1664]{1,0:T(8,128)(2,1)S(1)}, u32[]{:S(2)}, u32[]{:S(2)}) collective-permute-start(bf16[24,1664]{1,0:T(8,128)(2,1)S(1)} %get-tuple-element.40), channel_id=1, source_target_pairs={{0,6},{2,4},{4,2},{6,0},{8,14},{10,12},{12,10},{14,8},{16,22},{18,... | collective-permute-start | bytes 239624 | tf_op jit(solution)/shard_map/ppermute | solution.py:434
  43.8 0.5 collective-permute-start.11
  44.3 1.2 %collective-permute-start.12 = (bf16[24,1664]{1,0:T(8,128)(2,1)S(1)}, bf16[24,1664]{1,0:T(8,128)(2,1)S(1)}, u32[]{:S(2)}, u32[]{:S(2)}) collective-permute-start(bf16[24,1664]{1,0:T(8,128)(2,1)S(1)} %get-tuple-element.42), channel_id=1, source_target_pairs={{0,2},{2,0},{4,6},{6,4},{8,10},{10,8},{12,14},{14,12},{16,18},{18,... | collective-permute-start | bytes 239624 | tf_op jit(solution)/shard_map/ppermute | solution.py:434
  45.5 0.5 shard_map.36.refs_0_
  46.0 1.7 %collective-permute-done.10.refs_2_ = bf16[24,1664]{1,0:T(8,128)(2,1)S(1)} collective-permute-done((bf16[24,1664]{1,0:T(8,128)(2,1)S(1)}, bf16[24,1664]{1,0:T(8,128)(2,1)S(1)}, u32[]{:S(2)}, u32[]{:S(2)}) %collective-permute-start.10) | collective-permute-done | bytes 79904 | tf_op jit(solution)/shard_map/ppermute | solution.py:434
  47.7 0.8 %collective-permute-done.11.refs_3_ = bf16[24,1664]{1,0:T(8,128)(2,1)S(1)} collective-permute-done((bf16[24,1664]{1,0:T(8,128)(2,1)S(1)}, bf16[24,1664]{1,0:T(8,128)(2,1)S(1)}, u32[]{:S(2)}, u32[]{:S(2)}) %collective-permute-start.11) | collective-permute-done | bytes 79904 | tf_op jit(solution)/shard_map/ppermute | solution.py:434
  48.6 0.2 collective-permute-done.12.refs_4_
  48.8 0.5 shard_map.38
  49.3 3.7 %collective-permute-start.13 = (bf16[24,1408]{1,0:T(8,128)(2,1)S(1)}, bf16[24,1408]{1,0:T(8,128)(2,1)S(1)}, u32[]{:S(2)}, u32[]{:S(2)}) collective-permute-start(bf16[24,1408]{1,0:T(8,128)(2,1)S(1)} %get-tuple-element.44), channel_id=1, source_target_pairs={{0,24},{2,26},{4,28},{6,30},{8,16},{10,18},{12,20},{14,22},{16,8},... | collective-permute-start | bytes 202760 | tf_op jit(solution)/shard_map/ppermute | solution.py:434
  52.9 0.8 %collective-permute-start.15 = (bf16[24,1408]{1,0:T(8,128)(2,1)S(1)}, bf16[24,1408]{1,0:T(8,128)(2,1)S(1)}, u32[]{:S(2)}, u32[]{:S(2)}) collective-permute-start(bf16[24,1408]{1,0:T(8,128)(2,1)S(1)} %get-tuple-element.46), channel_id=1, source_target_pairs={{0,8},{2,10},{4,12},{6,14},{8,0},{10,2},{12,4},{14,6},{16,24},{18,... | collective-permute-start | bytes 202760 | tf_op jit(solution)/shard_map/ppermute | solution.py:434
  53.7 1.8 %collective-permute-done.13.refs_0_ = bf16[24,1408]{1,0:T(8,128)(2,1)S(1)} collective-permute-done((bf16[24,1408]{1,0:T(8,128)(2,1)S(1)}, bf16[24,1408]{1,0:T(8,128)(2,1)S(1)}, u32[]{:S(2)}, u32[]{:S(2)}) %collective-permute-start.13) | collective-permute-done | bytes 67616 | tf_op jit(solution)/shard_map/ppermute | solution.py:434
  55.5 2.6 %collective-permute-done.14.refs_1_ = bf16[24,1408]{1,0:T(8,128)(2,1)S(1)} collective-permute-done((bf16[24,1408]{1,0:T(8,128)(2,1)S(1)}, bf16[24,1408]{1,0:T(8,128)(2,1)S(1)}, u32[]{:S(2)}, u32[]{:S(2)}) %collective-permute-start.14) | collective-permute-done | bytes 67616 | tf_op jit(solution)/shard_map/ppermute | solution.py:434
  58.2 0.2 collective-permute-done.15.refs_2_
  58.4 0.8 %shard_map.39 = f32[3,10240]{1,0:T(4,128)} custom-call(f32[24,1280]{1,0:T(8,128)S(1)} %get-tuple-element.43.own_ref, bf16[24,1408]{1,0:T(8,128)(2,1)S(1)} %collective-permute-done.13.refs_0_, bf16[24,1408]{1,0:T(8,128)(2,1)S(1)} %collective-permute-done.14.refs_1_, bf16[24,1408]{1,0:T(8,128)(2,1)S(1)} %collective-permute-done.15.refs_2_), custom_call_target="tpu_custom_call" | custom-call | flops 1048576 | bytes 1048576 | tf_op jit(solution)/shard_map/pallas_call | solution.py:420
  (14 shorter events, 0.3 us)
Async XLA Ops:
  0.0 0.9 %copy-start = (bf16[3,16,1536]{2,1,0:T(8,128)(2,1)S(1)}, bf16[3,16,1536]{2,1,0:T(8,128)(2,1)}, u32[]{:S(2)}) copy-start(bf16[3,16,1536]{2,1,0:T(8,128)(2,1)} %in_ref.1) | copy-start | bytes 442372
  1.1 7.5 %collective-permute-start = (bf16[12,1536]{1,0:T(8,128)(2,1)S(1)}, bf16[12,1536]{1,0:T(8,128)(2,1)S(1)}, u32[]{:S(2)}, u32[]{:S(2)}) collective-permute-start(bf16[12,1536]{1,0:T(8,128)(2,1)S(1)} %get-tuple-element.27), channel_id=1, source_target_pairs={{0,6},{2,4},{4,2},{6,0},{8,14},{10,12},{12,10},{14,8},{16,22},{18,... | collective-permute-start | bytes 110600 | tf_op jit(solution)/shard_map/ppermute | solution.py:434
  5.1 4.1 %collective-permute-start.1 = (bf16[12,1536]{1,0:T(8,128)(2,1)S(1)}, bf16[12,1536]{1,0:T(8,128)(2,1)S(1)}, u32[]{:S(2)}, u32[]{:S(2)}) collective-permute-start(bf16[12,1536]{1,0:T(8,128)(2,1)S(1)} %get-tuple-element.28), channel_id=1, source_target_pairs={{0,4},{2,6},{4,0},{6,2},{8,12},{10,14},{12,8},{14,10},{16,20},{18,... | collective-permute-start | bytes 110600 | tf_op jit(solution)/shard_map/ppermute | solution.py:434
  5.6 4.1 %collective-permute-start.2 = (bf16[12,1536]{1,0:T(8,128)(2,1)S(1)}, bf16[12,1536]{1,0:T(8,128)(2,1)S(1)}, u32[]{:S(2)}, u32[]{:S(2)}) collective-permute-start(bf16[12,1536]{1,0:T(8,128)(2,1)S(1)} %get-tuple-element.29), channel_id=1, source_target_pairs={{0,2},{2,0},{4,6},{6,4},{8,10},{10,8},{12,14},{14,12},{16,18},{18,... | collective-permute-start | bytes 110600 | tf_op jit(solution)/shard_map/ppermute | solution.py:434
  10.0 9.3 %collective-permute-start.3 = (bf16[12,1536]{1,0:T(8,128)(2,1)S(1)}, bf16[12,1536]{1,0:T(8,128)(2,1)S(1)}, u32[]{:S(2)}, u32[]{:S(2)}) collective-permute-start(bf16[12,1536]{1,0:T(8,128)(2,1)S(1)} %get-tuple-element.31), channel_id=1, source_target_pairs={{0,24},{2,26},{4,28},{6,30},{8,16},{10,18},{12,20},{14,22},{16,8},... | collective-permute-start | bytes 110600 | tf_op jit(solution)/shard_map/ppermute | solution.py:434
  13.7 5.6 %collective-permute-start.4 = (bf16[12,1536]{1,0:T(8,128)(2,1)S(1)}, bf16[12,1536]{1,0:T(8,128)(2,1)S(1)}, u32[]{:S(2)}, u32[]{:S(2)}) collective-permute-start(bf16[12,1536]{1,0:T(8,128)(2,1)S(1)} %get-tuple-element.32), channel_id=1, source_target_pairs={{0,16},{2,18},{4,20},{6,22},{8,24},{10,26},{12,28},{14,30},{16,0},... | collective-permute-start | bytes 110600 | tf_op jit(solution)/shard_map/ppermute | solution.py:434
  13.7 5.6 %collective-permute-start.5 = (bf16[12,1536]{1,0:T(8,128)(2,1)S(1)}, bf16[12,1536]{1,0:T(8,128)(2,1)S(1)}, u32[]{:S(2)}, u32[]{:S(2)}) collective-permute-start(bf16[12,1536]{1,0:T(8,128)(2,1)S(1)} %get-tuple-element.33), channel_id=1, source_target_pairs={{0,8},{2,10},{4,12},{6,14},{8,0},{10,2},{12,4},{14,6},{16,24},{18,... | collective-permute-start | bytes 110600 | tf_op jit(solution)/shard_map/ppermute | solution.py:434
  19.6 2.0 %collective-permute-start.6 = (bf16[48,1536]{1,0:T(8,128)(2,1)S(1)}, bf16[48,1536]{1,0:T(8,128)(2,1)S(1)}, u32[]{:S(2)}, u32[]{:S(2)}) collective-permute-start(bf16[48,1536]{1,0:T(8,128)(2,1)S(1)} %shard_map.32.after_ref.refs_0_), channel_id=1, source_target_pairs={{0,1},{1,0},{2,3},{3,2},{4,5},{5,4},{6,7},{7,6},{8,9},{9,8},{10,11... | collective-permute-start | bytes 442376 | tf_op jit(solution)/shard_map/ppermute | solution.py:434
  32.4 11.9 %collective-permute-start.7 = (bf16[24,3712]{1,0:T(8,128)(2,1)S(1)}, bf16[24,3712]{1,0:T(8,128)(2,1)S(1)}, u32[]{:S(2)}, u32[]{:S(2)}) collective-permute-start(bf16[24,3712]{1,0:T(8,128)(2,1)S(1)} %get-tuple-element.35), channel_id=1, source_target_pairs={{0,6},{2,4},{4,2},{6,0},{8,14},{10,12},{12,10},{14,8},{16,22},{18,... | collective-permute-start | bytes 534536 | tf_op jit(solution)/shard_map/ppermute | solution.py:434
  34.3 11.2 %collective-permute-start.8 = (bf16[24,3712]{1,0:T(8,128)(2,1)S(1)}, bf16[24,3712]{1,0:T(8,128)(2,1)S(1)}, u32[]{:S(2)}, u32[]{:S(2)}) collective-permute-start(bf16[24,3712]{1,0:T(8,128)(2,1)S(1)} %get-tuple-element.36), channel_id=1, source_target_pairs={{0,4},{2,6},{4,0},{6,2},{8,12},{10,14},{12,8},{14,10},{16,20},{18,... | collective-permute-start | bytes 534536 | tf_op jit(solution)/shard_map/ppermute | solution.py:434
  34.8 10.7 %collective-permute-start.9 = (bf16[24,3712]{1,0:T(8,128)(2,1)S(1)}, bf16[24,3712]{1,0:T(8,128)(2,1)S(1)}, u32[]{:S(2)}, u32[]{:S(2)}) collective-permute-start(bf16[24,3712]{1,0:T(8,128)(2,1)S(1)} %get-tuple-element.37), channel_id=1, source_target_pairs={{0,2},{2,0},{4,6},{6,4},{8,10},{10,8},{12,14},{14,12},{16,18},{18,... | collective-permute-start | bytes 534536 | tf_op jit(solution)/shard_map/ppermute | solution.py:434
  41.9 5.8 %collective-permute-start.10 = (bf16[24,1664]{1,0:T(8,128)(2,1)S(1)}, bf16[24,1664]{1,0:T(8,128)(2,1)S(1)}, u32[]{:S(2)}, u32[]{:S(2)}) collective-permute-start(bf16[24,1664]{1,0:T(8,128)(2,1)S(1)} %get-tuple-element.40), channel_id=1, source_target_pairs={{0,6},{2,4},{4,2},{6,0},{8,14},{10,12},{12,10},{14,8},{16,22},{18,... | collective-permute-start | bytes 239624 | tf_op jit(solution)/shard_map/ppermute | solution.py:434
  43.8 4.7 %collective-permute-start.11 = (bf16[24,1664]{1,0:T(8,128)(2,1)S(1)}, bf16[24,1664]{1,0:T(8,128)(2,1)S(1)}, u32[]{:S(2)}, u32[]{:S(2)}) collective-permute-start(bf16[24,1664]{1,0:T(8,128)(2,1)S(1)} %get-tuple-element.41), channel_id=1, source_target_pairs={{0,4},{2,6},{4,0},{6,2},{8,12},{10,14},{12,8},{14,10},{16,20},{18,... | collective-permute-start | bytes 239624 | tf_op jit(solution)/shard_map/ppermute | solution.py:434
  44.3 4.4 %collective-permute-start.12 = (bf16[24,1664]{1,0:T(8,128)(2,1)S(1)}, bf16[24,1664]{1,0:T(8,128)(2,1)S(1)}, u32[]{:S(2)}, u32[]{:S(2)}) collective-permute-start(bf16[24,1664]{1,0:T(8,128)(2,1)S(1)} %get-tuple-element.42), channel_id=1, source_target_pairs={{0,2},{2,0},{4,6},{6,4},{8,10},{10,8},{12,14},{14,12},{16,18},{18,... | collective-permute-start | bytes 239624 | tf_op jit(solution)/shard_map/ppermute | solution.py:434
  49.3 6.3 %collective-permute-start.13 = (bf16[24,1408]{1,0:T(8,128)(2,1)S(1)}, bf16[24,1408]{1,0:T(8,128)(2,1)S(1)}, u32[]{:S(2)}, u32[]{:S(2)}) collective-permute-start(bf16[24,1408]{1,0:T(8,128)(2,1)S(1)} %get-tuple-element.44), channel_id=1, source_target_pairs={{0,24},{2,26},{4,28},{6,30},{8,16},{10,18},{12,20},{14,22},{16,8},... | collective-permute-start | bytes 202760 | tf_op jit(solution)/shard_map/ppermute | solution.py:434
  52.9 5.2 %collective-permute-start.14 = (bf16[24,1408]{1,0:T(8,128)(2,1)S(1)}, bf16[24,1408]{1,0:T(8,128)(2,1)S(1)}, u32[]{:S(2)}, u32[]{:S(2)}) collective-permute-start(bf16[24,1408]{1,0:T(8,128)(2,1)S(1)} %get-tuple-element.45), channel_id=1, source_target_pairs={{0,16},{2,18},{4,20},{6,22},{8,24},{10,26},{12,28},{14,30},{16,0},... | collective-permute-start | bytes 202760 | tf_op jit(solution)/shard_map/ppermute | solution.py:434
  52.9 5.5 %collective-permute-start.15 = (bf16[24,1408]{1,0:T(8,128)(2,1)S(1)}, bf16[24,1408]{1,0:T(8,128)(2,1)S(1)}, u32[]{:S(2)}, u32[]{:S(2)}) collective-permute-start(bf16[24,1408]{1,0:T(8,128)(2,1)S(1)} %get-tuple-element.46), channel_id=1, source_target_pairs={{0,8},{2,10},{4,12},{6,14},{8,0},{10,2},{12,4},{14,6},{16,24},{18,... | collective-permute-start | bytes 202760 | tf_op jit(solution)/shard_map/ppermute | solution.py:434

commit v4 on v3

--- a/solution.py
+++ b/solution.py
@@ -262,8 +262,7 @@
         for move in incoming[0]:
             move.start()
 
-        def tiles(chunk_ref, column, sums):
-            part, offset = divmod(column, width)
+        def tiles(chunk_ref, part, offset, sums):
             for at in range(0, unit, tile):
                 for place, values in multiply(window_ref, chunk_ref, at, tile, sums):
                     columns_at = pl.ds(offset + at + place, values.shape[1])
@@ -272,11 +271,31 @@
                         for begin, rows, where in packed_rows(group, r, part):
                             target[where : where + rows, columns_at] = values[begin : begin + rows]
 
+        def looped(sums):
+            for move in sum(incoming[1:], []):
+                move.start()
+
+            @pl.loop(0, len(held))
+            def _(k):
+                at = pl.multiple_of(k * unit, unit)
+                tiles(chunks[0].at[:, pl.ds(at, unit)], 0, at, sums)
+
+            part, offset = divmod(len(held) * unit, width)
+
+            @pl.loop(0, steps)
+            def _(k):
+                at = pl.multiple_of(k * unit, unit)
+                for move in copies(integral_ref, start + at, unit, ring.at[k], sems.at[k]):
+                    move.wait()
+                tiles(ring.at[k], part, offset + at, sums)
+
         def work(*sums):
             sets = [sums[:2], sums[2:]]
-            lead = len(held) if steps < SLOTS else 2
+            if len(chunks) == 1 and steps < SLOTS and not handed and (parts == 1 or len(held) == steps):
+                return looped(sets[0])
+            lead = 2
             for k in range(lead):
-                tiles(held[k], k * unit, sets[k % 2])
+                tiles(held[k], *divmod(k * unit, width), sets[k % 2])
                 for move in incoming[k + 1] if k + 1 < ahead else []:
                     move.start()
             for k in range(max(len(held) - lead, steps)):
@@ -285,9 +304,9 @@
                         move.wait()
                     for move in incoming[k + SLOTS - 1] if k + SLOTS - 1 < steps else []:
                         move.start()
-                    tiles(ring.at[k % SLOTS], (len(held) + k) * unit, sets[0])
+                    tiles(ring.at[k % SLOTS], *divmod((len(held) + k) * unit, width), sets[0])
                 if k + lead < len(held):
-                    tiles(held[k + lead], (k + lead) * unit, sets[1])
+                    tiles(held[k + lead], *divmod((k + lead) * unit, width), sets[1])
                 if k % 2 == 1 and k // 2 < len(handed):
                     for move in handed[k // 2]:
                         move.start()

time: 59.4 us -> 58.4 us (0.983)
  Pallas kernels: 29 us -> 27.9 us
    pallas_call x2, Pallas kernels: 16.6 us -> 15.5 us  [product(): pl.pallas_call(kernel, out_shape=shapes, in_specs=[pl.BlockSpec(memory_sp...]
  transfers between devices with their start and end apart: 16 -> 16, of which waited for: 8 -> 8; matrix products, arithmetic and copies ran while one was open for 0% -> 0% of each run, Pallas kernels for 27% -> 26%
where the time goes in v4:
time: 58.4 us; the launch traced here: 58.2 us
  Pallas kernels  27.9 us (48%)
  starting transfers between devices  20.7 us (35%)
  waiting for transfers between devices  8.6 us (15%)
  local copies, waits for them, and re-layouts  0.91 us (2%)
    ppermute x16, starting transfers between devices, swap(): return lax.ppermute(array, axis, [(i, i ^ by) for i in range(size)])  20.7 us
    pallas_call x2, Pallas kernels, product(): pl.pallas_call(kernel, out_shape=shapes, in_specs=[pl.BlockSpec(memory_sp...  15.5 us
    pallas_call x3, Pallas kernels, load(): pl.pallas_call(kernel, out_shape=pltpu.VMEM((depth, columns), BF16), in_s...  9.66 us
    ppermute x16, waiting for transfers between devices, swap(): return lax.ppermute(array, axis, [(i, i ^ by) for i in range(size)])  8.6 us
  transfers between devices with their start and end apart: 16, of which 8 were waited for; matrix products, arithmetic and copies ran while one was open for 0% of the time, Pallas kernels for 26%

profile of v4, /device:TPU:0, one launch (start us, length us, event | category | flops | bytes accessed | tf_op | source)
XLA Modules:
  0.0 58.2 jit_solution(17588652668670727054)
XLA Ops:
  0.0 0.9 %copy-done = bf16[3,16,1536]{2,1,0:T(8,128)(2,1)S(1)} copy-done((bf16[3,16,1536]{2,1,0:T(8,128)(2,1)S(1)}, bf16[3,16,1536]{2,1,0:T(8,128)(2,1)}, u32[]{:S(2)}) %copy-start) | copy-done | bytes 147480
  0.9 0.2 shard_map.28
  1.1 4.0 %collective-permute-start = (bf16[12,1536]{1,0:T(8,128)(2,1)S(1)}, bf16[12,1536]{1,0:T(8,128)(2,1)S(1)}, u32[]{:S(2)}, u32[]{:S(2)}) collective-permute-start(bf16[12,1536]{1,0:T(8,128)(2,1)S(1)} %get-tuple-element.27), channel_id=1, source_target_pairs={{0,6},{2,4},{4,2},{6,0},{8,14},{10,12},{12,10},{14,8},{16,22},{18,... | collective-permute-start | bytes 110600 | tf_op jit(solution)/shard_map/ppermute | solution.py:453
  5.1 0.5 collective-permute-start.1
  5.6 0.1 collective-permute-start.2
  5.7 2.9 %shard_map.29.refs_4_.refs_0_ = bf16[3072,1024]{1,0:T(8,128)(2,1)S(1)} custom-call(bf16[3072,10240]{1,0:T(8,128)(2,1)} %integral_ref.9, bf16[12,1536]{1,0:T(8,128)(2,1)S(1)} %get-tuple-element.26.after_ref.refs_0_), custom_call_target="tpu_custom_call" | custom-call | bytes 6291456 | tf_op jit(solution)/shard_map/pallas_call | solution.py:59
  8.6 0.5 collective-permute-done.1.refs_2_
  9.2 0.5 collective-permute-done.2.refs_3_
  9.7 0.3 shard_map.30
  10.0 3.7 %collective-permute-start.3 = (bf16[12,1536]{1,0:T(8,128)(2,1)S(1)}, bf16[12,1536]{1,0:T(8,128)(2,1)S(1)}, u32[]{:S(2)}, u32[]{:S(2)}) collective-permute-start(bf16[12,1536]{1,0:T(8,128)(2,1)S(1)} %get-tuple-element.31), channel_id=1, source_target_pairs={{0,24},{2,26},{4,28},{6,30},{8,16},{10,18},{12,20},{14,22},{16,8},... | collective-permute-start | bytes 110600 | tf_op jit(solution)/shard_map/ppermute | solution.py:453
  13.7 0.8 %collective-permute-start.5 = (bf16[12,1536]{1,0:T(8,128)(2,1)S(1)}, bf16[12,1536]{1,0:T(8,128)(2,1)S(1)}, u32[]{:S(2)}, u32[]{:S(2)}) collective-permute-start(bf16[12,1536]{1,0:T(8,128)(2,1)S(1)} %get-tuple-element.33), channel_id=1, source_target_pairs={{0,8},{2,10},{4,12},{6,14},{8,0},{10,2},{12,4},{14,6},{16,24},{18,... | collective-permute-start | bytes 110600 | tf_op jit(solution)/shard_map/ppermute | solution.py:453
  14.5 4.8 %shard_map.31.refs_4_.refs_1_ = bf16[3072,2048]{1,0:T(8,128)(2,1)S(1)} custom-call(bf16[3072,10240]{1,0:T(8,128)(2,1)} %integral_ref.9, bf16[12,1536]{1,0:T(8,128)(2,1)S(1)} %get-tuple-element.30.after_ref.refs_0_), custom_call_target="tpu_custom_call" | custom-call | bytes 12582912 | tf_op jit(solution)/shard_map/pallas_call | solution.py:59
  19.3 0.3 shard_map.32.after_ref.refs_0_
  19.7 1.9 %shard_map.33.refs_2_ = bf16[3072,512]{1,0:T(8,128)(2,1)S(1)} custom-call(bf16[3072,10240]{1,0:T(8,128)(2,1)} %integral_ref.9, bf16[48,1536]{1,0:T(8,128)(2,1)S(1)} %shard_map.32.after_ref.refs_0_), custom_call_target="tpu_custom_call" | custom-call | bytes 3145728 | tf_op jit(solution)/shard_map/pallas_call | solution.py:59
  21.7 10.7 %shard_map.35 = (f32[24,3584]{1,0:T(8,128)S(1)}, bf16[24,3712]{1,0:T(8,128)(2,1)S(1)}, bf16[24,3712]{1,0:T(8,128)(2,1)S(1)}, bf16[24,3712]{1,0:T(8,128)(2,1)S(1)}, bf16[3072,1536]{1,0:T(8,128)(2,1)S(1)}) custom-call(bf16[48,3072]{1,0:T(8,128)(2,1)S(1)} %shard_map.34.window_ref, bf16[3072,10240]{1,0:T(8,128)(2,1)} %integral_ref.9, ...), custom_call_target="tpu_custom_call" | custom-call | flops 2113929216 | bytes 44040192 | tf_op jit(solution)/shard_map/pallas_call | solution.py:336
  32.4 1.9 %collective-permute-start.7 = (bf16[24,3712]{1,0:T(8,128)(2,1)S(1)}, bf16[24,3712]{1,0:T(8,128)(2,1)S(1)}, u32[]{:S(2)}, u32[]{:S(2)}) collective-permute-start(bf16[24,3712]{1,0:T(8,128)(2,1)S(1)} %get-tuple-element.35), channel_id=1, source_target_pairs={{0,6},{2,4},{4,2},{6,0},{8,14},{10,12},{12,10},{14,8},{16,22},{18,... | collective-permute-start | bytes 534536 | tf_op jit(solution)/shard_map/ppermute | solution.py:453
  34.3 0.5 collective-permute-start.8
  34.8 1.2 %collective-permute-start.9 = (bf16[24,3712]{1,0:T(8,128)(2,1)S(1)}, bf16[24,3712]{1,0:T(8,128)(2,1)S(1)}, u32[]{:S(2)}, u32[]{:S(2)}) collective-permute-start(bf16[24,3712]{1,0:T(8,128)(2,1)S(1)} %get-tuple-element.37), channel_id=1, source_target_pairs={{0,2},{2,0},{4,6},{6,4},{8,10},{10,8},{12,14},{14,12},{16,18},{18,... | collective-permute-start | bytes 534536 | tf_op jit(solution)/shard_map/ppermute | solution.py:453
  36.0 4.8 %shard_map.37 = (f32[24,1536]{1,0:T(8,128)S(1)}, bf16[24,1664]{1,0:T(8,128)(2,1)S(1)}, bf16[24,1664]{1,0:T(8,128)(2,1)S(1)}, bf16[24,1664]{1,0:T(8,128)(2,1)S(1)}) custom-call(bf16[48,3072]{1,0:T(8,128)(2,1)S(1)} %shard_map.34.window_ref, bf16[3072,10240]{1,0:T(8,128)(2,1)} %integral_ref.9, bf16[3072,1536]{1,0:T(8,128)(2,1)S(1)} %get-tuple-element.38.refs_0_, ...), custom_call_target="tpu_custom_call" | custom-call | flops 905969664 | bytes 18874368 | tf_op jit(solution)/shard_map/pallas_call | solution.py:336
  40.8 1.9 %collective-permute-start.10 = (bf16[24,1664]{1,0:T(8,128)(2,1)S(1)}, bf16[24,1664]{1,0:T(8,128)(2,1)S(1)}, u32[]{:S(2)}, u32[]{:S(2)}) collective-permute-start(bf16[24,1664]{1,0:T(8,128)(2,1)S(1)} %get-tuple-element.40), channel_id=1, source_target_pairs={{0,6},{2,4},{4,2},{6,0},{8,14},{10,12},{12,10},{14,8},{16,22},{18,... | collective-permute-start | bytes 239624 | tf_op jit(solution)/shard_map/ppermute | solution.py:453
  42.7 0.5 collective-permute-start.11
  43.2 1.2 %collective-permute-start.12 = (bf16[24,1664]{1,0:T(8,128)(2,1)S(1)}, bf16[24,1664]{1,0:T(8,128)(2,1)S(1)}, u32[]{:S(2)}, u32[]{:S(2)}) collective-permute-start(bf16[24,1664]{1,0:T(8,128)(2,1)S(1)} %get-tuple-element.42), channel_id=1, source_target_pairs={{0,2},{2,0},{4,6},{6,4},{8,10},{10,8},{12,14},{14,12},{16,18},{18,... | collective-permute-start | bytes 239624 | tf_op jit(solution)/shard_map/ppermute | solution.py:453
  44.4 0.5 shard_map.36.refs_0_
  44.9 1.7 %collective-permute-done.10.refs_2_ = bf16[24,1664]{1,0:T(8,128)(2,1)S(1)} collective-permute-done((bf16[24,1664]{1,0:T(8,128)(2,1)S(1)}, bf16[24,1664]{1,0:T(8,128)(2,1)S(1)}, u32[]{:S(2)}, u32[]{:S(2)}) %collective-permute-start.10) | collective-permute-done | bytes 79904 | tf_op jit(solution)/shard_map/ppermute | solution.py:453
  46.6 1.0 %collective-permute-done.11.refs_3_ = bf16[24,1664]{1,0:T(8,128)(2,1)S(1)} collective-permute-done((bf16[24,1664]{1,0:T(8,128)(2,1)S(1)}, bf16[24,1664]{1,0:T(8,128)(2,1)S(1)}, u32[]{:S(2)}, u32[]{:S(2)}) %collective-permute-start.11) | collective-permute-done | bytes 79904 | tf_op jit(solution)/shard_map/ppermute | solution.py:453
  47.7 0.5 shard_map.38
  48.2 3.7 %collective-permute-start.13 = (bf16[24,1408]{1,0:T(8,128)(2,1)S(1)}, bf16[24,1408]{1,0:T(8,128)(2,1)S(1)}, u32[]{:S(2)}, u32[]{:S(2)}) collective-permute-start(bf16[24,1408]{1,0:T(8,128)(2,1)S(1)} %get-tuple-element.44), channel_id=1, source_target_pairs={{0,24},{2,26},{4,28},{6,30},{8,16},{10,18},{12,20},{14,22},{16,8},... | collective-permute-start | bytes 202760 | tf_op jit(solution)/shard_map/ppermute | solution.py:453
  51.8 0.8 %collective-permute-start.15 = (bf16[24,1408]{1,0:T(8,128)(2,1)S(1)}, bf16[24,1408]{1,0:T(8,128)(2,1)S(1)}, u32[]{:S(2)}, u32[]{:S(2)}) collective-permute-start(bf16[24,1408]{1,0:T(8,128)(2,1)S(1)} %get-tuple-element.46), channel_id=1, source_target_pairs={{0,8},{2,10},{4,12},{6,14},{8,0},{10,2},{12,4},{14,6},{16,24},{18,... | collective-permute-start | bytes 202760 | tf_op jit(solution)/shard_map/ppermute | solution.py:453
  52.6 1.9 %collective-permute-done.13.refs_0_ = bf16[24,1408]{1,0:T(8,128)(2,1)S(1)} collective-permute-done((bf16[24,1408]{1,0:T(8,128)(2,1)S(1)}, bf16[24,1408]{1,0:T(8,128)(2,1)S(1)}, u32[]{:S(2)}, u32[]{:S(2)}) %collective-permute-start.13) | collective-permute-done | bytes 67616 | tf_op jit(solution)/shard_map/ppermute | solution.py:453
  54.5 2.7 %collective-permute-done.14.refs_1_ = bf16[24,1408]{1,0:T(8,128)(2,1)S(1)} collective-permute-done((bf16[24,1408]{1,0:T(8,128)(2,1)S(1)}, bf16[24,1408]{1,0:T(8,128)(2,1)S(1)}, u32[]{:S(2)}, u32[]{:S(2)}) %collective-permute-start.14) | collective-permute-done | bytes 67616 | tf_op jit(solution)/shard_map/ppermute | solution.py:453
  57.3 0.1 collective-permute-done.15.refs_2_
  57.4 0.8 %shard_map.39 = f32[3,10240]{1,0:T(4,128)} custom-call(f32[24,1280]{1,0:T(8,128)S(1)} %get-tuple-element.43.own_ref, bf16[24,1408]{1,0:T(8,128)(2,1)S(1)} %collective-permute-done.13.refs_0_, bf16[24,1408]{1,0:T(8,128)(2,1)S(1)} %collective-permute-done.14.refs_1_, bf16[24,1408]{1,0:T(8,128)(2,1)S(1)} %collective-permute-done.15.refs_2_), custom_call_target="tpu_custom_call" | custom-call | flops 1048576 | bytes 1048576 | tf_op jit(solution)/shard_map/pallas_call | solution.py:439
  (14 shorter events, 0.2 us)
Async XLA Ops:
  0.0 0.9 %copy-start = (bf16[3,16,1536]{2,1,0:T(8,128)(2,1)S(1)}, bf16[3,16,1536]{2,1,0:T(8,128)(2,1)}, u32[]{:S(2)}) copy-start(bf16[3,16,1536]{2,1,0:T(8,128)(2,1)} %in_ref.1) | copy-start | bytes 442372
  1.1 7.5 %collective-permute-start = (bf16[12,1536]{1,0:T(8,128)(2,1)S(1)}, bf16[12,1536]{1,0:T(8,128)(2,1)S(1)}, u32[]{:S(2)}, u32[]{:S(2)}) collective-permute-start(bf16[12,1536]{1,0:T(8,128)(2,1)S(1)} %get-tuple-element.27), channel_id=1, source_target_pairs={{0,6},{2,4},{4,2},{6,0},{8,14},{10,12},{12,10},{14,8},{16,22},{18,... | collective-permute-start | bytes 110600 | tf_op jit(solution)/shard_map/ppermute | solution.py:453
  5.1 4.1 %collective-permute-start.1 = (bf16[12,1536]{1,0:T(8,128)(2,1)S(1)}, bf16[12,1536]{1,0:T(8,128)(2,1)S(1)}, u32[]{:S(2)}, u32[]{:S(2)}) collective-permute-start(bf16[12,1536]{1,0:T(8,128)(2,1)S(1)} %get-tuple-element.28), channel_id=1, source_target_pairs={{0,4},{2,6},{4,0},{6,2},{8,12},{10,14},{12,8},{14,10},{16,20},{18,... | collective-permute-start | bytes 110600 | tf_op jit(solution)/shard_map/ppermute | solution.py:453
  5.6 4.1 %collective-permute-start.2 = (bf16[12,1536]{1,0:T(8,128)(2,1)S(1)}, bf16[12,1536]{1,0:T(8,128)(2,1)S(1)}, u32[]{:S(2)}, u32[]{:S(2)}) collective-permute-start(bf16[12,1536]{1,0:T(8,128)(2,1)S(1)} %get-tuple-element.29), channel_id=1, source_target_pairs={{0,2},{2,0},{4,6},{6,4},{8,10},{10,8},{12,14},{14,12},{16,18},{18,... | collective-permute-start | bytes 110600 | tf_op jit(solution)/shard_map/ppermute | solution.py:453
  10.0 9.3 %collective-permute-start.3 = (bf16[12,1536]{1,0:T(8,128)(2,1)S(1)}, bf16[12,1536]{1,0:T(8,128)(2,1)S(1)}, u32[]{:S(2)}, u32[]{:S(2)}) collective-permute-start(bf16[12,1536]{1,0:T(8,128)(2,1)S(1)} %get-tuple-element.31), channel_id=1, source_target_pairs={{0,24},{2,26},{4,28},{6,30},{8,16},{10,18},{12,20},{14,22},{16,8},... | collective-permute-start | bytes 110600 | tf_op jit(solution)/shard_map/ppermute | solution.py:453
  13.7 5.6 %collective-permute-start.4 = (bf16[12,1536]{1,0:T(8,128)(2,1)S(1)}, bf16[12,1536]{1,0:T(8,128)(2,1)S(1)}, u32[]{:S(2)}, u32[]{:S(2)}) collective-permute-start(bf16[12,1536]{1,0:T(8,128)(2,1)S(1)} %get-tuple-element.32), channel_id=1, source_target_pairs={{0,16},{2,18},{4,20},{6,22},{8,24},{10,26},{12,28},{14,30},{16,0},... | collective-permute-start | bytes 110600 | tf_op jit(solution)/shard_map/ppermute | solution.py:453
  13.7 5.6 %collective-permute-start.5 = (bf16[12,1536]{1,0:T(8,128)(2,1)S(1)}, bf16[12,1536]{1,0:T(8,128)(2,1)S(1)}, u32[]{:S(2)}, u32[]{:S(2)}) collective-permute-start(bf16[12,1536]{1,0:T(8,128)(2,1)S(1)} %get-tuple-element.33), channel_id=1, source_target_pairs={{0,8},{2,10},{4,12},{6,14},{8,0},{10,2},{12,4},{14,6},{16,24},{18,... | collective-permute-start | bytes 110600 | tf_op jit(solution)/shard_map/ppermute | solution.py:453
  19.6 2.0 %collective-permute-start.6 = (bf16[48,1536]{1,0:T(8,128)(2,1)S(1)}, bf16[48,1536]{1,0:T(8,128)(2,1)S(1)}, u32[]{:S(2)}, u32[]{:S(2)}) collective-permute-start(bf16[48,1536]{1,0:T(8,128)(2,1)S(1)} %shard_map.32.after_ref.refs_0_), channel_id=1, source_target_pairs={{0,1},{1,0},{2,3},{3,2},{4,5},{5,4},{6,7},{7,6},{8,9},{9,8},{10,11... | collective-permute-start | bytes 442376 | tf_op jit(solution)/shard_map/ppermute | solution.py:453
  32.4 10.8 %collective-permute-start.7 = (bf16[24,3712]{1,0:T(8,128)(2,1)S(1)}, bf16[24,3712]{1,0:T(8,128)(2,1)S(1)}, u32[]{:S(2)}, u32[]{:S(2)}) collective-permute-start(bf16[24,3712]{1,0:T(8,128)(2,1)S(1)} %get-tuple-element.35), channel_id=1, source_target_pairs={{0,6},{2,4},{4,2},{6,0},{8,14},{10,12},{12,10},{14,8},{16,22},{18,... | collective-permute-start | bytes 534536 | tf_op jit(solution)/shard_map/ppermute | solution.py:453
  34.3 10.1 %collective-permute-start.8 = (bf16[24,3712]{1,0:T(8,128)(2,1)S(1)}, bf16[24,3712]{1,0:T(8,128)(2,1)S(1)}, u32[]{:S(2)}, u32[]{:S(2)}) collective-permute-start(bf16[24,3712]{1,0:T(8,128)(2,1)S(1)} %get-tuple-element.36), channel_id=1, source_target_pairs={{0,4},{2,6},{4,0},{6,2},{8,12},{10,14},{12,8},{14,10},{16,20},{18,... | collective-permute-start | bytes 534536 | tf_op jit(solution)/shard_map/ppermute | solution.py:453
  34.8 9.6 %collective-permute-start.9 = (bf16[24,3712]{1,0:T(8,128)(2,1)S(1)}, bf16[24,3712]{1,0:T(8,128)(2,1)S(1)}, u32[]{:S(2)}, u32[]{:S(2)}) collective-permute-start(bf16[24,3712]{1,0:T(8,128)(2,1)S(1)} %get-tuple-element.37), channel_id=1, source_target_pairs={{0,2},{2,0},{4,6},{6,4},{8,10},{10,8},{12,14},{14,12},{16,18},{18,... | collective-permute-start | bytes 534536 | tf_op jit(solution)/shard_map/ppermute | solution.py:453
  40.8 5.8 %collective-permute-start.10 = (bf16[24,1664]{1,0:T(8,128)(2,1)S(1)}, bf16[24,1664]{1,0:T(8,128)(2,1)S(1)}, u32[]{:S(2)}, u32[]{:S(2)}) collective-permute-start(bf16[24,1664]{1,0:T(8,128)(2,1)S(1)} %get-tuple-element.40), channel_id=1, source_target_pairs={{0,6},{2,4},{4,2},{6,0},{8,14},{10,12},{12,10},{14,8},{16,22},{18,... | collective-permute-start | bytes 239624 | tf_op jit(solution)/shard_map/ppermute | solution.py:453
  42.7 4.8 %collective-permute-start.11 = (bf16[24,1664]{1,0:T(8,128)(2,1)S(1)}, bf16[24,1664]{1,0:T(8,128)(2,1)S(1)}, u32[]{:S(2)}, u32[]{:S(2)}) collective-permute-start(bf16[24,1664]{1,0:T(8,128)(2,1)S(1)} %get-tuple-element.41), channel_id=1, source_target_pairs={{0,4},{2,6},{4,0},{6,2},{8,12},{10,14},{12,8},{14,10},{16,20},{18,... | collective-permute-start | bytes 239624 | tf_op jit(solution)/shard_map/ppermute | solution.py:453
  43.2 4.4 %collective-permute-start.12 = (bf16[24,1664]{1,0:T(8,128)(2,1)S(1)}, bf16[24,1664]{1,0:T(8,128)(2,1)S(1)}, u32[]{:S(2)}, u32[]{:S(2)}) collective-permute-start(bf16[24,1664]{1,0:T(8,128)(2,1)S(1)} %get-tuple-element.42), channel_id=1, source_target_pairs={{0,2},{2,0},{4,6},{6,4},{8,10},{10,8},{12,14},{14,12},{16,18},{18,... | collective-permute-start | bytes 239624 | tf_op jit(solution)/shard_map/ppermute | solution.py:453
  48.2 6.4 %collective-permute-start.13 = (bf16[24,1408]{1,0:T(8,128)(2,1)S(1)}, bf16[24,1408]{1,0:T(8,128)(2,1)S(1)}, u32[]{:S(2)}, u32[]{:S(2)}) collective-permute-start(bf16[24,1408]{1,0:T(8,128)(2,1)S(1)} %get-tuple-element.44), channel_id=1, source_target_pairs={{0,24},{2,26},{4,28},{6,30},{8,16},{10,18},{12,20},{14,22},{16,8},... | collective-permute-start | bytes 202760 | tf_op jit(solution)/shard_map/ppermute | solution.py:453
  51.8 5.4 %collective-permute-start.14 = (bf16[24,1408]{1,0:T(8,128)(2,1)S(1)}, bf16[24,1408]{1,0:T(8,128)(2,1)S(1)}, u32[]{:S(2)}, u32[]{:S(2)}) collective-permute-start(bf16[24,1408]{1,0:T(8,128)(2,1)S(1)} %get-tuple-element.45), channel_id=1, source_target_pairs={{0,16},{2,18},{4,20},{6,22},{8,24},{10,26},{12,28},{14,30},{16,0},... | collective-permute-start | bytes 202760 | tf_op jit(solution)/shard_map/ppermute | solution.py:453
  51.8 5.6 %collective-permute-start.15 = (bf16[24,1408]{1,0:T(8,128)(2,1)S(1)}, bf16[24,1408]{1,0:T(8,128)(2,1)S(1)}, u32[]{:S(2)}, u32[]{:S(2)}) collective-permute-start(bf16[24,1408]{1,0:T(8,128)(2,1)S(1)} %get-tuple-element.46), channel_id=1, source_target_pairs={{0,8},{2,10},{4,12},{6,14},{8,0},{10,2},{12,4},{14,6},{16,24},{18,... | collective-permute-start | bytes 202760 | tf_op jit(solution)/shard_map/ppermute | solution.py:453

commit v5 on v4

--- a/solution.py
+++ b/solution.py
@@ -16,7 +16,7 @@
 SECOND = 6
 MORE = 3
 SLOTS = 4
-PIECES = 4
+PIECES = 2
 TILE = 512
 MATRIX = 256
 LANES = 128

time: 58.4 us -> 58.3 us (level)
  no operation moved by 1% of the time
where the time goes in v5:
time: 58.3 us; the launch traced here: 58.1 us
  Pallas kernels  27.8 us (48%)
  starting transfers between devices  20.7 us (36%)
  waiting for transfers between devices  8.65 us (15%)
  local copies, waits for them, and re-layouts  0.91 us (2%)
    ppermute x16, starting transfers between devices, swap(): return lax.ppermute(array, axis, [(i, i ^ by) for i in range(size)])  20.7 us
    pallas_call x2, Pallas kernels, product(): pl.pallas_call(kernel, out_shape=shapes, in_specs=[pl.BlockSpec(memory_sp...  15.4 us
    pallas_call x3, Pallas kernels, load(): pl.pallas_call(kernel, out_shape=pltpu.VMEM((depth, columns), BF16), in_s...  9.61 us
    ppermute x16, waiting for transfers between devices, swap(): return lax.ppermute(array, axis, [(i, i ^ by) for i in range(size)])  8.65 us
  transfers between devices with their start and end apart: 16, of which 8 were waited for; matrix products, arithmetic and copies ran while one was open for 0% of the time, Pallas kernels for 26%

profile of v5, /device:TPU:0, one launch (start us, length us, event | category | flops | bytes accessed | tf_op | source)
XLA Modules:
  0.0 58.1 jit_solution(2468334996785367082)
XLA Ops:
  0.0 0.9 %copy-done = bf16[3,16,1536]{2,1,0:T(8,128)(2,1)S(1)} copy-done((bf16[3,16,1536]{2,1,0:T(8,128)(2,1)S(1)}, bf16[3,16,1536]{2,1,0:T(8,128)(2,1)}, u32[]{:S(2)}) %copy-start) | copy-done | bytes 147480
  0.9 0.2 shard_map.28
  1.1 4.0 %collective-permute-start = (bf16[12,1536]{1,0:T(8,128)(2,1)S(1)}, bf16[12,1536]{1,0:T(8,128)(2,1)S(1)}, u32[]{:S(2)}, u32[]{:S(2)}) collective-permute-start(bf16[12,1536]{1,0:T(8,128)(2,1)S(1)} %get-tuple-element.27), channel_id=1, source_target_pairs={{0,6},{2,4},{4,2},{6,0},{8,14},{10,12},{12,10},{14,8},{16,22},{18,... | collective-permute-start | bytes 110600 | tf_op jit(solution)/shard_map/ppermute | solution.py:453
  5.1 0.5 collective-permute-start.1
  5.6 0.1 collective-permute-start.2
  5.7 2.9 %shard_map.29.refs_4_.refs_0_ = bf16[3072,1024]{1,0:T(8,128)(2,1)S(1)} custom-call(bf16[3072,10240]{1,0:T(8,128)(2,1)} %integral_ref.9, bf16[12,1536]{1,0:T(8,128)(2,1)S(1)} %get-tuple-element.26.after_ref.refs_0_), custom_call_target="tpu_custom_call" | custom-call | bytes 6291456 | tf_op jit(solution)/shard_map/pallas_call | solution.py:59
  8.6 0.5 collective-permute-done.1.refs_2_
  9.2 0.5 collective-permute-done.2.refs_3_
  9.7 0.3 shard_map.30
  10.0 3.7 %collective-permute-start.3 = (bf16[12,1536]{1,0:T(8,128)(2,1)S(1)}, bf16[12,1536]{1,0:T(8,128)(2,1)S(1)}, u32[]{:S(2)}, u32[]{:S(2)}) collective-permute-start(bf16[12,1536]{1,0:T(8,128)(2,1)S(1)} %get-tuple-element.31), channel_id=1, source_target_pairs={{0,24},{2,26},{4,28},{6,30},{8,16},{10,18},{12,20},{14,22},{16,8},... | collective-permute-start | bytes 110600 | tf_op jit(solution)/shard_map/ppermute | solution.py:453
  13.7 0.8 %collective-permute-start.5 = (bf16[12,1536]{1,0:T(8,128)(2,1)S(1)}, bf16[12,1536]{1,0:T(8,128)(2,1)S(1)}, u32[]{:S(2)}, u32[]{:S(2)}) collective-permute-start(bf16[12,1536]{1,0:T(8,128)(2,1)S(1)} %get-tuple-element.33), channel_id=1, source_target_pairs={{0,8},{2,10},{4,12},{6,14},{8,0},{10,2},{12,4},{14,6},{16,24},{18,... | collective-permute-start | bytes 110600 | tf_op jit(solution)/shard_map/ppermute | solution.py:453
  14.5 4.8 %shard_map.31.refs_4_.refs_1_ = bf16[3072,2048]{1,0:T(8,128)(2,1)S(1)} custom-call(bf16[3072,10240]{1,0:T(8,128)(2,1)} %integral_ref.9, bf16[12,1536]{1,0:T(8,128)(2,1)S(1)} %get-tuple-element.30.after_ref.refs_0_), custom_call_target="tpu_custom_call" | custom-call | bytes 12582912 | tf_op jit(solution)/shard_map/pallas_call | solution.py:59
  19.3 0.3 shard_map.32.after_ref.refs_0_
  19.7 1.9 %shard_map.33.refs_2_ = bf16[3072,512]{1,0:T(8,128)(2,1)S(1)} custom-call(bf16[3072,10240]{1,0:T(8,128)(2,1)} %integral_ref.9, bf16[48,1536]{1,0:T(8,128)(2,1)S(1)} %shard_map.32.after_ref.refs_0_), custom_call_target="tpu_custom_call" | custom-call | bytes 3145728 | tf_op jit(solution)/shard_map/pallas_call | solution.py:59
  21.7 10.6 %shard_map.35 = (f32[24,3584]{1,0:T(8,128)S(1)}, bf16[24,3712]{1,0:T(8,128)(2,1)S(1)}, bf16[24,3712]{1,0:T(8,128)(2,1)S(1)}, bf16[24,3712]{1,0:T(8,128)(2,1)S(1)}, bf16[3072,1536]{1,0:T(8,128)(2,1)S(1)}) custom-call(bf16[48,3072]{1,0:T(8,128)(2,1)S(1)} %shard_map.34.window_ref, bf16[3072,10240]{1,0:T(8,128)(2,1)} %integral_ref.9, ...), custom_call_target="tpu_custom_call" | custom-call | flops 2113929216 | bytes 44040192 | tf_op jit(solution)/shard_map/pallas_call | solution.py:336
  32.3 1.9 %collective-permute-start.7 = (bf16[24,3712]{1,0:T(8,128)(2,1)S(1)}, bf16[24,3712]{1,0:T(8,128)(2,1)S(1)}, u32[]{:S(2)}, u32[]{:S(2)}) collective-permute-start(bf16[24,3712]{1,0:T(8,128)(2,1)S(1)} %get-tuple-element.35), channel_id=1, source_target_pairs={{0,6},{2,4},{4,2},{6,0},{8,14},{10,12},{12,10},{14,8},{16,22},{18,... | collective-permute-start | bytes 534536 | tf_op jit(solution)/shard_map/ppermute | solution.py:453
  34.2 0.5 collective-permute-start.8
  34.7 1.1 %collective-permute-start.9 = (bf16[24,3712]{1,0:T(8,128)(2,1)S(1)}, bf16[24,3712]{1,0:T(8,128)(2,1)S(1)}, u32[]{:S(2)}, u32[]{:S(2)}) collective-permute-start(bf16[24,3712]{1,0:T(8,128)(2,1)S(1)} %get-tuple-element.37), channel_id=1, source_target_pairs={{0,2},{2,0},{4,6},{6,4},{8,10},{10,8},{12,14},{14,12},{16,18},{18,... | collective-permute-start | bytes 534536 | tf_op jit(solution)/shard_map/ppermute | solution.py:453
  35.9 4.8 %shard_map.37 = (f32[24,1536]{1,0:T(8,128)S(1)}, bf16[24,1664]{1,0:T(8,128)(2,1)S(1)}, bf16[24,1664]{1,0:T(8,128)(2,1)S(1)}, bf16[24,1664]{1,0:T(8,128)(2,1)S(1)}) custom-call(bf16[48,3072]{1,0:T(8,128)(2,1)S(1)} %shard_map.34.window_ref, bf16[3072,10240]{1,0:T(8,128)(2,1)} %integral_ref.9, bf16[3072,1536]{1,0:T(8,128)(2,1)S(1)} %get-tuple-element.38.refs_0_, ...), custom_call_target="tpu_custom_call" | custom-call | flops 905969664 | bytes 18874368 | tf_op jit(solution)/shard_map/pallas_call | solution.py:336
  40.7 1.9 %collective-permute-start.10 = (bf16[24,1664]{1,0:T(8,128)(2,1)S(1)}, bf16[24,1664]{1,0:T(8,128)(2,1)S(1)}, u32[]{:S(2)}, u32[]{:S(2)}) collective-permute-start(bf16[24,1664]{1,0:T(8,128)(2,1)S(1)} %get-tuple-element.40), channel_id=1, source_target_pairs={{0,6},{2,4},{4,2},{6,0},{8,14},{10,12},{12,10},{14,8},{16,22},{18,... | collective-permute-start | bytes 239624 | tf_op jit(solution)/shard_map/ppermute | solution.py:453
  42.6 0.5 collective-permute-start.11
  43.1 1.1 %collective-permute-start.12 = (bf16[24,1664]{1,0:T(8,128)(2,1)S(1)}, bf16[24,1664]{1,0:T(8,128)(2,1)S(1)}, u32[]{:S(2)}, u32[]{:S(2)}) collective-permute-start(bf16[24,1664]{1,0:T(8,128)(2,1)S(1)} %get-tuple-element.42), channel_id=1, source_target_pairs={{0,2},{2,0},{4,6},{6,4},{8,10},{10,8},{12,14},{14,12},{16,18},{18,... | collective-permute-start | bytes 239624 | tf_op jit(solution)/shard_map/ppermute | solution.py:453
  44.2 0.5 shard_map.36.refs_0_
  44.7 1.7 %collective-permute-done.10.refs_2_ = bf16[24,1664]{1,0:T(8,128)(2,1)S(1)} collective-permute-done((bf16[24,1664]{1,0:T(8,128)(2,1)S(1)}, bf16[24,1664]{1,0:T(8,128)(2,1)S(1)}, u32[]{:S(2)}, u32[]{:S(2)}) %collective-permute-start.10) | collective-permute-done | bytes 79904 | tf_op jit(solution)/shard_map/ppermute | solution.py:453
  46.5 1.0 %collective-permute-done.11.refs_3_ = bf16[24,1664]{1,0:T(8,128)(2,1)S(1)} collective-permute-done((bf16[24,1664]{1,0:T(8,128)(2,1)S(1)}, bf16[24,1664]{1,0:T(8,128)(2,1)S(1)}, u32[]{:S(2)}, u32[]{:S(2)}) %collective-permute-start.11) | collective-permute-done | bytes 79904 | tf_op jit(solution)/shard_map/ppermute | solution.py:453
  47.5 0.5 shard_map.38
  48.0 3.7 %collective-permute-start.13 = (bf16[24,1408]{1,0:T(8,128)(2,1)S(1)}, bf16[24,1408]{1,0:T(8,128)(2,1)S(1)}, u32[]{:S(2)}, u32[]{:S(2)}) collective-permute-start(bf16[24,1408]{1,0:T(8,128)(2,1)S(1)} %get-tuple-element.44), channel_id=1, source_target_pairs={{0,24},{2,26},{4,28},{6,30},{8,16},{10,18},{12,20},{14,22},{16,8},... | collective-permute-start | bytes 202760 | tf_op jit(solution)/shard_map/ppermute | solution.py:453
  51.7 0.8 %collective-permute-start.15 = (bf16[24,1408]{1,0:T(8,128)(2,1)S(1)}, bf16[24,1408]{1,0:T(8,128)(2,1)S(1)}, u32[]{:S(2)}, u32[]{:S(2)}) collective-permute-start(bf16[24,1408]{1,0:T(8,128)(2,1)S(1)} %get-tuple-element.46), channel_id=1, source_target_pairs={{0,8},{2,10},{4,12},{6,14},{8,0},{10,2},{12,4},{14,6},{16,24},{18,... | collective-permute-start | bytes 202760 | tf_op jit(solution)/shard_map/ppermute | solution.py:453
  52.5 1.9 %collective-permute-done.13.refs_0_ = bf16[24,1408]{1,0:T(8,128)(2,1)S(1)} collective-permute-done((bf16[24,1408]{1,0:T(8,128)(2,1)S(1)}, bf16[24,1408]{1,0:T(8,128)(2,1)S(1)}, u32[]{:S(2)}, u32[]{:S(2)}) %collective-permute-start.13) | collective-permute-done | bytes 67616 | tf_op jit(solution)/shard_map/ppermute | solution.py:453
  54.5 2.7 %collective-permute-done.14.refs_1_ = bf16[24,1408]{1,0:T(8,128)(2,1)S(1)} collective-permute-done((bf16[24,1408]{1,0:T(8,128)(2,1)S(1)}, bf16[24,1408]{1,0:T(8,128)(2,1)S(1)}, u32[]{:S(2)}, u32[]{:S(2)}) %collective-permute-start.14) | collective-permute-done | bytes 67616 | tf_op jit(solution)/shard_map/ppermute | solution.py:453
  57.2 0.1 collective-permute-done.15.refs_2_
  57.3 0.8 %shard_map.39 = f32[3,10240]{1,0:T(4,128)} custom-call(f32[24,1280]{1,0:T(8,128)S(1)} %get-tuple-element.43.own_ref, bf16[24,1408]{1,0:T(8,128)(2,1)S(1)} %collective-permute-done.13.refs_0_, bf16[24,1408]{1,0:T(8,128)(2,1)S(1)} %collective-permute-done.14.refs_1_, bf16[24,1408]{1,0:T(8,128)(2,1)S(1)} %collective-permute-done.15.refs_2_), custom_call_target="tpu_custom_call" | custom-call | flops 1048576 | bytes 1048576 | tf_op jit(solution)/shard_map/pallas_call | solution.py:439
  (14 shorter events, 0.2 us)
Async XLA Ops:
  0.0 0.9 %copy-start = (bf16[3,16,1536]{2,1,0:T(8,128)(2,1)S(1)}, bf16[3,16,1536]{2,1,0:T(8,128)(2,1)}, u32[]{:S(2)}) copy-start(bf16[3,16,1536]{2,1,0:T(8,128)(2,1)} %in_ref.1) | copy-start | bytes 442372
  1.1 7.5 %collective-permute-start = (bf16[12,1536]{1,0:T(8,128)(2,1)S(1)}, bf16[12,1536]{1,0:T(8,128)(2,1)S(1)}, u32[]{:S(2)}, u32[]{:S(2)}) collective-permute-start(bf16[12,1536]{1,0:T(8,128)(2,1)S(1)} %get-tuple-element.27), channel_id=1, source_target_pairs={{0,6},{2,4},{4,2},{6,0},{8,14},{10,12},{12,10},{14,8},{16,22},{18,... | collective-permute-start | bytes 110600 | tf_op jit(solution)/shard_map/ppermute | solution.py:453
  5.1 4.1 %collective-permute-start.1 = (bf16[12,1536]{1,0:T(8,128)(2,1)S(1)}, bf16[12,1536]{1,0:T(8,128)(2,1)S(1)}, u32[]{:S(2)}, u32[]{:S(2)}) collective-permute-start(bf16[12,1536]{1,0:T(8,128)(2,1)S(1)} %get-tuple-element.28), channel_id=1, source_target_pairs={{0,4},{2,6},{4,0},{6,2},{8,12},{10,14},{12,8},{14,10},{16,20},{18,... | collective-permute-start | bytes 110600 | tf_op jit(solution)/shard_map/ppermute | solution.py:453
  5.6 4.1 %collective-permute-start.2 = (bf16[12,1536]{1,0:T(8,128)(2,1)S(1)}, bf16[12,1536]{1,0:T(8,128)(2,1)S(1)}, u32[]{:S(2)}, u32[]{:S(2)}) collective-permute-start(bf16[12,1536]{1,0:T(8,128)(2,1)S(1)} %get-tuple-element.29), channel_id=1, source_target_pairs={{0,2},{2,0},{4,6},{6,4},{8,10},{10,8},{12,14},{14,12},{16,18},{18,... | collective-permute-start | bytes 110600 | tf_op jit(solution)/shard_map/ppermute | solution.py:453
  10.0 9.2 %collective-permute-start.3 = (bf16[12,1536]{1,0:T(8,128)(2,1)S(1)}, bf16[12,1536]{1,0:T(8,128)(2,1)S(1)}, u32[]{:S(2)}, u32[]{:S(2)}) collective-permute-start(bf16[12,1536]{1,0:T(8,128)(2,1)S(1)} %get-tuple-element.31), channel_id=1, source_target_pairs={{0,24},{2,26},{4,28},{6,30},{8,16},{10,18},{12,20},{14,22},{16,8},... | collective-permute-start | bytes 110600 | tf_op jit(solution)/shard_map/ppermute | solution.py:453
  13.7 5.6 %collective-permute-start.4 = (bf16[12,1536]{1,0:T(8,128)(2,1)S(1)}, bf16[12,1536]{1,0:T(8,128)(2,1)S(1)}, u32[]{:S(2)}, u32[]{:S(2)}) collective-permute-start(bf16[12,1536]{1,0:T(8,128)(2,1)S(1)} %get-tuple-element.32), channel_id=1, source_target_pairs={{0,16},{2,18},{4,20},{6,22},{8,24},{10,26},{12,28},{14,30},{16,0},... | collective-permute-start | bytes 110600 | tf_op jit(solution)/shard_map/ppermute | solution.py:453
  13.7 5.6 %collective-permute-start.5 = (bf16[12,1536]{1,0:T(8,128)(2,1)S(1)}, bf16[12,1536]{1,0:T(8,128)(2,1)S(1)}, u32[]{:S(2)}, u32[]{:S(2)}) collective-permute-start(bf16[12,1536]{1,0:T(8,128)(2,1)S(1)} %get-tuple-element.33), channel_id=1, source_target_pairs={{0,8},{2,10},{4,12},{6,14},{8,0},{10,2},{12,4},{14,6},{16,24},{18,... | collective-permute-start | bytes 110600 | tf_op jit(solution)/shard_map/ppermute | solution.py:453
  19.6 2.0 %collective-permute-start.6 = (bf16[48,1536]{1,0:T(8,128)(2,1)S(1)}, bf16[48,1536]{1,0:T(8,128)(2,1)S(1)}, u32[]{:S(2)}, u32[]{:S(2)}) collective-permute-start(bf16[48,1536]{1,0:T(8,128)(2,1)S(1)} %shard_map.32.after_ref.refs_0_), channel_id=1, source_target_pairs={{0,1},{1,0},{2,3},{3,2},{4,5},{5,4},{6,7},{7,6},{8,9},{9,8},{10,11... | collective-permute-start | bytes 442376 | tf_op jit(solution)/shard_map/ppermute | solution.py:453
  32.3 10.8 %collective-permute-start.7 = (bf16[24,3712]{1,0:T(8,128)(2,1)S(1)}, bf16[24,3712]{1,0:T(8,128)(2,1)S(1)}, u32[]{:S(2)}, u32[]{:S(2)}) collective-permute-start(bf16[24,3712]{1,0:T(8,128)(2,1)S(1)} %get-tuple-element.35), channel_id=1, source_target_pairs={{0,6},{2,4},{4,2},{6,0},{8,14},{10,12},{12,10},{14,8},{16,22},{18,... | collective-permute-start | bytes 534536 | tf_op jit(solution)/shard_map/ppermute | solution.py:453
  34.2 10.0 %collective-permute-start.8 = (bf16[24,3712]{1,0:T(8,128)(2,1)S(1)}, bf16[24,3712]{1,0:T(8,128)(2,1)S(1)}, u32[]{:S(2)}, u32[]{:S(2)}) collective-permute-start(bf16[24,3712]{1,0:T(8,128)(2,1)S(1)} %get-tuple-element.36), channel_id=1, source_target_pairs={{0,4},{2,6},{4,0},{6,2},{8,12},{10,14},{12,8},{14,10},{16,20},{18,... | collective-permute-start | bytes 534536 | tf_op jit(solution)/shard_map/ppermute | solution.py:453
  34.7 9.5 %collective-permute-start.9 = (bf16[24,3712]{1,0:T(8,128)(2,1)S(1)}, bf16[24,3712]{1,0:T(8,128)(2,1)S(1)}, u32[]{:S(2)}, u32[]{:S(2)}) collective-permute-start(bf16[24,3712]{1,0:T(8,128)(2,1)S(1)} %get-tuple-element.37), channel_id=1, source_target_pairs={{0,2},{2,0},{4,6},{6,4},{8,10},{10,8},{12,14},{14,12},{16,18},{18,... | collective-permute-start | bytes 534536 | tf_op jit(solution)/shard_map/ppermute | solution.py:453
  40.7 5.8 %collective-permute-start.10 = (bf16[24,1664]{1,0:T(8,128)(2,1)S(1)}, bf16[24,1664]{1,0:T(8,128)(2,1)S(1)}, u32[]{:S(2)}, u32[]{:S(2)}) collective-permute-start(bf16[24,1664]{1,0:T(8,128)(2,1)S(1)} %get-tuple-element.40), channel_id=1, source_target_pairs={{0,6},{2,4},{4,2},{6,0},{8,14},{10,12},{12,10},{14,8},{16,22},{18,... | collective-permute-start | bytes 239624 | tf_op jit(solution)/shard_map/ppermute | solution.py:453
  42.6 4.9 %collective-permute-start.11 = (bf16[24,1664]{1,0:T(8,128)(2,1)S(1)}, bf16[24,1664]{1,0:T(8,128)(2,1)S(1)}, u32[]{:S(2)}, u32[]{:S(2)}) collective-permute-start(bf16[24,1664]{1,0:T(8,128)(2,1)S(1)} %get-tuple-element.41), channel_id=1, source_target_pairs={{0,4},{2,6},{4,0},{6,2},{8,12},{10,14},{12,8},{14,10},{16,20},{18,... | collective-permute-start | bytes 239624 | tf_op jit(solution)/shard_map/ppermute | solution.py:453
  43.1 4.4 %collective-permute-start.12 = (bf16[24,1664]{1,0:T(8,128)(2,1)S(1)}, bf16[24,1664]{1,0:T(8,128)(2,1)S(1)}, u32[]{:S(2)}, u32[]{:S(2)}) collective-permute-start(bf16[24,1664]{1,0:T(8,128)(2,1)S(1)} %get-tuple-element.42), channel_id=1, source_target_pairs={{0,2},{2,0},{4,6},{6,4},{8,10},{10,8},{12,14},{14,12},{16,18},{18,... | collective-permute-start | bytes 239624 | tf_op jit(solution)/shard_map/ppermute | solution.py:453
  48.0 6.4 %collective-permute-start.13 = (bf16[24,1408]{1,0:T(8,128)(2,1)S(1)}, bf16[24,1408]{1,0:T(8,128)(2,1)S(1)}, u32[]{:S(2)}, u32[]{:S(2)}) collective-permute-start(bf16[24,1408]{1,0:T(8,128)(2,1)S(1)} %get-tuple-element.44), channel_id=1, source_target_pairs={{0,24},{2,26},{4,28},{6,30},{8,16},{10,18},{12,20},{14,22},{16,8},... | collective-permute-start | bytes 202760 | tf_op jit(solution)/shard_map/ppermute | solution.py:453
  51.7 5.5 %collective-permute-start.14 = (bf16[24,1408]{1,0:T(8,128)(2,1)S(1)}, bf16[24,1408]{1,0:T(8,128)(2,1)S(1)}, u32[]{:S(2)}, u32[]{:S(2)}) collective-permute-start(bf16[24,1408]{1,0:T(8,128)(2,1)S(1)} %get-tuple-element.45), channel_id=1, source_target_pairs={{0,16},{2,18},{4,20},{6,22},{8,24},{10,26},{12,28},{14,30},{16,0},... | collective-permute-start | bytes 202760 | tf_op jit(solution)/shard_map/ppermute | solution.py:453
  51.7 5.6 %collective-permute-start.15 = (bf16[24,1408]{1,0:T(8,128)(2,1)S(1)}, bf16[24,1408]{1,0:T(8,128)(2,1)S(1)}, u32[]{:S(2)}, u32[]{:S(2)}) collective-permute-start(bf16[24,1408]{1,0:T(8,128)(2,1)S(1)} %get-tuple-element.46), channel_id=1, source_target_pairs={{0,8},{2,10},{4,12},{6,14},{8,0},{10,2},{12,4},{14,6},{16,24},{18,... | collective-permute-start | bytes 202760 | tf_op jit(solution)/shard_map/ppermute | solution.py:453
